TPU v7x, 256 devices: a whole 4x4x8 slice. The times are simulated.
256 devices in a mesh: row: 16 (over z, core), col: 16 (over y, x).
Axes of the slice: x: 4, y: 4, z: 8, core: 2. Of those that a mesh axis runs over, the one named last changes fastest.
Arguments:
- tokens: bfloat16 [1024, 12288], P('col', 'row'), may hold values from -120 to 120, as said below
- norm_gain: float32 [12288], P('row'), may hold values from 0.1 to 1.9
- norm_bias: float32 [12288], P('row'), may hold values from -3 to 3
- weight_in: bfloat16 [12288, 49152], P('row', 'col'), may hold values from -0.0546875 to 0.0546875
- bias_in: float32 [49152], P('col'), may hold values from -3 to 3
- weight_out: bfloat16 [49152, 12288], P('col', 'row'), may hold values from -0.02734375 to 0.02734375
- bias_out: float32 [12288], P('row'), may hold values from -3 to 3
Outputs:
- block_out: bfloat16 [1024, 12288], P('col', 'row')
Inputs may be any that keep to these rules, and one draw needn't show every extreme that they name: `tokens`: real-valued activations.
All inputs are finite; a program needn't handle non-finite values.
Results may differ from a plain program's by a relative error of at most 0.0075.
Values may be sent and summed in bfloat16 or wider, within the bound.
No kernel may reach another device: no remote copies, remote signals or barrier semaphores. Data moves between devices by JAX's collectives and lax.ppermute only.
A program may use at most 64 MiB of HBM per device.

v0:
```python
import functools

import jax
import jax.numpy as jnp
from jax import lax
from jax.experimental import pallas as pl
from jax.experimental.pallas import tpu as pltpu
from jax.sharding import Mesh
from jax.sharding import PartitionSpec as P

epsilon = 1e-05
planes = 8
parts = 2
group = 8
rows = 32
plane = ("y", "x")
megabyte = 2**20
whole = pl.BlockSpec(memory_space=pltpu.VMEM)
scalars = pl.BlockSpec(memory_space=pltpu.SMEM)
anywhere = pl.BlockSpec(memory_space=pl.ANY)


def swap(value):
    return lax.ppermute(value, "core", [(0, 1), (1, 0)])


def onward(value, distance=1):
    pairs = []
    for z in range(planes):
        pairs.append((2 * z, 2 * ((z + distance) % planes)))
        pairs.append((2 * z + 1, 2 * ((z - distance) % planes) + 1))
    return lax.ppermute(value, ("z", "core"), pairs)


def around(z, steps):
    return lax.rem(z + steps + planes, planes)


def near_and_far(z, core):
    way = 1 - 2 * core
    out = [(0, core), (0, 1 - core)]
    for steps in (1, 2, 3):
        out += [(-way * steps, core), (-way * steps, 1 - core)]
    out.append((4, core))
    for steps in (1, 2, 3):
        out += [(way * steps, 1 - core), (way * steps, core)]
    out.append((4, 1 - core))
    return [2 * around(z, steps) + which for steps, which in out]


def params(size):
    return pltpu.CompilerParams(vmem_limit_bytes=size * megabyte)


def copies_kernel(offsets, place, tokens, *refs):
    out = refs[-1]
    for slot, steps in enumerate(offsets):
        block = tokens[around(place[0], steps)]
        for i in range(out.shape[0]):
            out[i, slot] = block


def copies(offsets, place, tokens, *before):
    shape = (16, len(offsets)) + tokens.shape[1:]
    return pl.pallas_call(
        functools.partial(copies_kernel, offsets),
        in_specs=[scalars, whole] + [anywhere] * len(before),
        out_specs=whole,
        out_shape=jax.ShapeDtypeStruct(shape, tokens.dtype),
        compiler_params=params(16),
    )(place, tokens, *before)


def tops_kernel(gain, bias, weight, *refs):
    out = refs[-1]
    left = []
    for value in (gain[...], bias[...]):
        for _ in range(3):
            piece = value.astype(jnp.bfloat16).astype(jnp.float32)
            left.append(piece)
            value = value - piece
    left += [jnp.zeros_like(left[0])] * 10
    left = jnp.concatenate(left).astype(jnp.bfloat16)
    value = jnp.dot(left, weight[...], preferred_element_type=jnp.float32)
    out[0:1] = value[0:1] + value[1:2] + value[2:3]
    out[1:2] = value[3:4] + value[4:5] + value[5:6]


def tops_product(gain, bias, weight, *before):
    features, units = weight.shape
    step = 1536
    return pl.pallas_call(
        tops_kernel,
        grid=(units // step,),
        in_specs=[pl.BlockSpec((1, features), lambda i: (0, 0))] * 2
        + [pl.BlockSpec((features, step), lambda i: (0, i))]
        + [anywhere] * len(before),
        out_specs=pl.BlockSpec((2, step), lambda i: (0, i)),
        out_shape=jax.ShapeDtypeStruct((2, units), jnp.float32),
        compiler_params=params(24),
        cost_estimate=pl.CostEstimate(
            flops=32 * features * units, bytes_accessed=2 * features * units, transcendentals=0
        ),
    )(gain, bias, weight, *before)


def early_blocks(core):
    theirs, ours = [], []
    for part in range(parts):
        theirs += [(0, part, 1 - core), (2 - core, part, 1 - core), (2 - core, part, core)]
        ours += [(0, part, core), (1 + core, part, core), (1 + core, part, 1 - core)]
    return theirs, ours


def later_blocks(core):
    theirs, ours = [], []
    for part in range(parts):
        for first in (3, 5):
            theirs += [(first + 1 - core, part, 1 - core), (first + 1 - core, part, core)]
            ours += [(first + core, part, core), (first + core, part, 1 - core)]
        ours += [(7, part, core), (7, part, 1 - core)]
    return theirs, ours


def first_kernel(choose, place, gathered, gain, weight, *refs):
    theirs, ours, left, notes = refs[-4:]
    z, core = place[0], place[1]
    features = gathered.shape[-1]
    split = theirs.shape[0]

    lane = lax.broadcasted_iota(jnp.int32, (rows, 128), 1)
    kind = lax.div(lane, 16)
    here = lane - 16 * kind == 2 * z + core
    for slot, (number, part, which) in enumerate(sum(choose(core), [])):
        span = slice(slot * rows, (slot + 1) * rows)
        base = 8 * part + 4 * which
        block = jnp.concatenate(
            [gathered[base + i, number].astype(jnp.float32) for i in range(4)]
        )
        mean = jnp.sum(block, axis=1, keepdims=True) / features
        differ = block - mean
        left[span] = (differ * gain[...]).astype(jnp.bfloat16)
        note = jnp.zeros((rows, 128), jnp.float32)
        squares = jnp.sum(differ * differ, axis=1, keepdims=True)
        for first, value in ((0, mean), (3, squares)):
            rest = jnp.broadcast_to(value, (rows, 128))
            for piece in range(3):
                near = rest.astype(jnp.bfloat16).astype(jnp.float32)
                note = jnp.where(kind == first + piece, near, note)
                rest = rest - near
        notes[span] = jnp.where(here, note, 0.0).astype(jnp.bfloat16)
    theirs[:, -128:] = notes[:split]
    ours[:, -128:] = notes[split:]

    def work(span):
        value = jnp.dot(left[...], weight[:, span], preferred_element_type=jnp.float32)
        theirs[:, span] = value[:split].astype(jnp.bfloat16)
        ours[:, span] = value[split:].astype(jnp.bfloat16)

    columns(weight.shape[1], 768, work)


def first_product(choose, place, gathered, gain, weight, *before):
    features, units = weight.shape
    split, rest = (rows * len(blocks) for blocks in choose(0))
    tokens = split + rest
    return pl.pallas_call(
        functools.partial(first_kernel, choose),
        in_specs=[scalars] + [whole] * 3 + [anywhere] * len(before),
        out_specs=[whole, whole],
        out_shape=[
            jax.ShapeDtypeStruct((split, units + 128), jnp.bfloat16),
            jax.ShapeDtypeStruct((rest, units + 128), jnp.bfloat16),
        ],
        scratch_shapes=[
            pltpu.VMEM((tokens, features), jnp.bfloat16),
            pltpu.VMEM((tokens, 128), jnp.bfloat16),
        ],
        compiler_params=params(24),
        cost_estimate=pl.CostEstimate(
            flops=2 * tokens * features * units,
            bytes_accessed=2 * (features * units + tokens * (features + units)),
            transcendentals=0,
        ),
    )(place, gathered, gain, weight, *before)


def columns(wide, step, work):
    def chunk(number, carry):
        work(pl.ds(pl.multiple_of(number * step, step), step))
        return carry

    lax.fori_loop(0, wide // step, chunk, 0)


def sum_kernel(number, first, second, ours, theirs, moving, *refs):
    out = refs[-1]
    size = out.shape[0]

    def work(span):
        total = ours[first * rows : first * rows + size, span].astype(jnp.float32)
        if number == 4:
            total = total + moving[rows:, span].astype(jnp.float32)
        else:
            share = theirs[second * rows : second * rows + size, span]
            total = total + share.astype(jnp.float32)
        if number in (2, 3):
            total = total + moving[:, span].astype(jnp.float32)
        if number == 1:
            near = total[:rows] + moving[:, span].astype(jnp.float32)
            out[:rows, span] = near.astype(jnp.bfloat16)
            out[rows:, span] = total[rows:].astype(jnp.bfloat16)
        else:
            out[:, span] = total.astype(jnp.bfloat16)

    columns(out.shape[1], 640, work)


def ring_sum(number, first, second, ours, theirs, moving, *before):
    shape = (rows if number in (0, 4) else 2 * rows, ours.shape[1])
    return pl.pallas_call(
        functools.partial(sum_kernel, number, first, second),
        in_specs=[whole] * 3 + [anywhere] * len(before),
        out_specs=whole,
        out_shape=jax.ShapeDtypeStruct(shape, jnp.bfloat16),
        compiler_params=params(16),
        cost_estimate=pl.CostEstimate(
            flops=3 * shape[0] * shape[1], bytes_accessed=8 * shape[0] * shape[1], transcendentals=0
        ),
    )(ours, theirs, moving, *before)


def activate_kernel(features, first, place, ours, moving, other, *refs):
    tops, bias, out = refs[:-2], refs[-2], refs[-1]
    units = out.shape[1]

    def sums(span):
        total = ours[first * rows : (first + 1) * rows, span].astype(jnp.float32)
        total = total + moving[:rows, span].astype(jnp.float32)
        return total + other[:, span].astype(jnp.float32)

    notes = sums(pl.ds(units, 128))
    lane = lax.broadcasted_iota(jnp.int32, (rows, 128), 1)
    kind = lax.div(lane, 16)
    lane = lane - 16 * kind
    tops = [top.at[i] for top in tops for i in range(top.shape[0])]
    means, squares = [], 0.0
    for number in near_and_far(place[0], place[1]):
        mine = jnp.where(lane == number, notes, 0.0)
        means.append(jnp.sum(jnp.where(kind < 3, mine, 0.0), axis=1, keepdims=True))
        squares = squares + jnp.sum(jnp.where(kind >= 3, mine, 0.0), axis=1, keepdims=True)
    center = sum(means) / len(means)
    away = [mean - center for mean in means]
    for value in away:
        squares = squares + features * value * value
    scale = lax.rsqrt(squares / (len(means) * features) + epsilon)

    def work(span):
        moved, biases = 0.0, bias[:, span]
        for value, top in zip(away, tops):
            moved = moved + value * top[0:1, span]
            biases = biases + top[1:2, span]
        preact = (sums(span) + moved) * scale + biases
        out[:, span] = jax.nn.gelu(preact, approximate=True).astype(jnp.bfloat16)

    columns(units, 512, work)


def activate(features, first, place, ours, moving, other, tops, bias):
    units = bias.shape[1]
    return pl.pallas_call(
        functools.partial(activate_kernel, features, first),
        in_specs=[scalars] + [whole] * 7,
        out_specs=whole,
        out_shape=jax.ShapeDtypeStruct((rows, units), jnp.bfloat16),
        compiler_params=params(24),
        cost_estimate=pl.CostEstimate(
            flops=60 * rows * units, bytes_accessed=12 * rows * units, transcendentals=rows * units
        ),
    )(place, ours, moving, other, *tops, bias)


def pass_kernel(value, *refs):
    out = refs[-1]
    out[...] = value[: out.shape[0]]


def passed(value, tokens, *before):
    return pl.pallas_call(
        pass_kernel,
        in_specs=[whole] + [anywhere] * len(before),
        out_specs=whole,
        out_shape=jax.ShapeDtypeStruct((tokens, value.shape[1]), value.dtype),
        compiler_params=params(16),
    )(value, *before)


def product_kernel(*refs):
    tiles, weight, out = refs[:-2], refs[-2], refs[-1]
    left = jnp.concatenate([tile[...] for tile in tiles])
    total = jnp.dot(left, weight[...], preferred_element_type=jnp.float32)
    out[...] = total.astype(jnp.bfloat16)


def merge_kernel(slots, earlier, place, *refs):
    done, weight, out, left = refs[0], refs[earlier], refs[-2], refs[-1]
    first = 0
    for tile in refs[earlier + 1 : -2]:
        left[first : first + tile.shape[0]] = tile[...]
        first += tile.shape[0]
    places = [(early, 8 * part + 4 * which, number) for early, (number, part, which) in slots(place[1])]

    def work(span):
        total = jnp.dot(left[...], weight[:, span], preferred_element_type=jnp.float32)
        old = new = 0
        for early, base, number in places:
            for i in range(4):
                if early:
                    first = old * rows + i * group
                    out[base + i, number, :, span] = done[first : first + group, span]
                else:
                    first = new * rows + i * group
                    out[base + i, number, :, span] = total[first : first + group].astype(jnp.bfloat16)
            old, new = old + early, new + 1 - early

    columns(weight.shape[1], 256, work)


def near_slots(core):
    out = []
    for part in range(parts):
        out += [(0, (0, part, core)), (0, (0, part, 1 - core))]
        for steps in (1, 2):
            number = 2 * steps - 1 + core
            out += [(0, (number, part, core)), (0, (number, part, 1 - core))]
        for steps in (1, 2):
            number = 2 * steps - core
            out += [(0, (number, part, 1 - core)), (0, (number, part, core))]
    return out


def far_slots(core):
    out = []
    for part in range(parts):
        out += [(1, (core, part, core)), (1, (core, part, 1 - core))]
        out += [(1, (1 - core, part, 1 - core)), (1, (1 - core, part, core))]
    for part in range(parts):
        out += [(0, (2, part, core)), (0, (2, part, 1 - core))]
    return out


def second_cost(tokens, weight):
    units, features = weight.shape
    return pl.CostEstimate(
        flops=2 * tokens * features * units,
        bytes_accessed=2 * (features * units + tokens * (features + units)),
        transcendentals=0,
    )


def second_product(tiles, weight):
    tokens = sum(tile.shape[0] for tile in tiles)
    return pl.pallas_call(
        product_kernel,
        in_specs=[whole] * (len(tiles) + 1),
        out_specs=whole,
        out_shape=jax.ShapeDtypeStruct((tokens, weight.shape[1]), jnp.bfloat16),
        compiler_params=params(24),
        cost_estimate=second_cost(tokens, weight),
    )(*tiles, weight)


def merged_product(slots, groups, place, done, tiles, weight, *before):
    tokens = sum(tile.shape[0] for tile in tiles)

    def kernel(*refs):
        skipped = len(refs) - 2 - len(before)
        merge_kernel(slots, len(done), *refs[:skipped], *refs[-2:])

    return pl.pallas_call(
        kernel,
        in_specs=[scalars] + [whole] * (len(done) + 1 + len(tiles)) + [anywhere] * len(before),
        out_specs=whole,
        out_shape=jax.ShapeDtypeStruct((16, groups, group, weight.shape[1]), jnp.bfloat16),
        scratch_shapes=[pltpu.VMEM((tokens, weight.shape[0]), jnp.bfloat16)],
        compiler_params=params(24),
        cost_estimate=second_cost(tokens, weight),
    )(place, *done, weight, *tiles, *before)


def base_kernel(tokens, bias, out):
    for i in range(tokens.shape[0]):
        out[i] = tokens[i].astype(jnp.float32) + bias[...]


def base_sum(tokens, bias):
    return pl.pallas_call(
        base_kernel,
        in_specs=[whole] * 2,
        out_specs=whole,
        out_shape=jax.ShapeDtypeStruct(tokens.shape, jnp.float32),
        compiler_params=params(16),
    )(tokens, bias)


def last_kernel(place, near, far, base, out):
    offsets = (0, -1, 1, -2, 2, -3, 3, 4)
    for slot, steps in enumerate(offsets):
        where = around(place[0], steps)
        shares, number = (near, slot) if slot < 5 else (far, slot - 5)

        def more(i, total):
            return total + shares[i, number].astype(jnp.float32)

        total = lax.fori_loop(0, shares.shape[0], more, base[where])
        out[where] = total.astype(jnp.bfloat16)


def last_sum(place, near, far, base):
    return pl.pallas_call(
        last_kernel,
        in_specs=[scalars] + [whole] * 3,
        out_specs=whole,
        out_shape=jax.ShapeDtypeStruct(base.shape, jnp.bfloat16),
        compiler_params=params(24),
    )(place, near, far, base)


def body(tokens, norm_gain, norm_bias, weight_in, bias_in, weight_out, bias_out):
    core, z = lax.axis_index("core"), lax.axis_index("z")
    place = jnp.stack([z, core]).astype(jnp.int32)
    features = tokens.shape[1]
    norm_gain, norm_bias = norm_gain.reshape(1, -1), norm_bias.reshape(1, -1)
    bias_in, bias_out = bias_in.reshape(1, -1), bias_out.reshape(1, -1)
    grouped = tokens.reshape(planes, group, features)

    def exchange(value):
        return lax.all_to_all(value, plane, 0, 0, tiled=True)

    ready = copies((4, 3, -3, 2, -2, 1, -1, 0), place, grouped)
    gathered = exchange(ready)
    mine = tops_product(norm_gain, norm_bias, weight_in, ready)
    pair = jnp.stack([mine, swap(mine)])
    near = [onward(pair, distance) for distance in (1, 2, 3)] + [onward(mine, 4)[None]]
    near = jnp.concatenate(near)
    far = swap(near)
    tops = pair, near, far

    theirs, ours = first_product(early_blocks, place, gathered, norm_gain, weight_in, far)
    theirs_later, ours_later = first_product(
        later_blocks, place, gathered, norm_gain, weight_in, theirs
    )
    theirs = swap(theirs)
    sent = [ring_sum(0, 3 * part, 3 * part, ours, theirs, theirs) for part in range(parts)]
    moving = [onward(value) for value in sent]
    for part in range(parts):
        first = 3 * part + 1
        moving[part] = onward(ring_sum(1, first, first, ours, theirs, moving[part]))
    theirs, ours = swap(theirs_later), ours_later
    hidden = []
    for part in range(parts):
        first, second = 6 * part, 4 * part
        step = moving[part]
        step = onward(ring_sum(2, first, second, ours, theirs, step))
        step = onward(ring_sum(3, first + 2, second + 2, ours, theirs, step))
        other = swap(ring_sum(4, first + 5, 0, ours, theirs, step))
        hidden.append(activate(features, first + 4, place, ours, step, other, tops, bias_in))

    base = base_sum(grouped, bias_out)
    tiles, steps = [], []
    for part in range(parts):
        step = jnp.concatenate([hidden[part], swap(hidden[part])])
        own = [step]
        for _ in range(2):
            step = onward(step)
            own.append(step)
        tiles += own + [swap(value) for value in own[1:]]
        steps.append(onward(step))
    near = merged_product(near_slots, 5, place, [], tiles, weight_out, base)
    four = [onward(passed(value, rows, near)) for value in steps]
    near = exchange(near)
    done = second_product([value for step in steps for value in (step, swap(step))], weight_out)
    four = [passed(value, rows, done) for value in four]
    far = [value for step in four for value in (step, swap(step))]
    far = merged_product(far_slots, 3, place, [done], far, weight_out)
    far = exchange(far)
    out = last_sum(place, near, far, base)
    return out.reshape(tokens.shape)


def solution(mesh):
    fine = Mesh(mesh.devices.reshape(8, 2, 4, 4), ("z", "core", "y", "x"))
    row, col = ("z", "core"), ("y", "x")
    placed = (P(col, row), P(row), P(row), P(row, col), P(col), P(col, row), P(row))
    return jax.shard_map(
        body, mesh=fine, in_specs=placed, out_specs=P(col, row), check_vma=False
    )
```

profile of v0, /device:TPU:1, one launch (start us, length us, event | category | flops | bytes accessed | tf_op | source)
XLA Modules:
  0.0 162.7 jit_solution(13270190290742475630)
XLA Ops:
  2.8 7.7 %all-to-all-start = ((bf16[16,8,8,768]{3,2,1,0:T(8,128)(2,1)}), bf16[16,8,8,768]{3,2,1,0:T(8,128)(2,1)S(1)}, u32[]{:S(2)}, u32[]{:S(2)}) async-start(bf16[16,8,8,768]{3,2,1,0:T(8,128)(2,1)} %shard_map.73.refs_0_), calls=%async_computation | async-start | bytes 3145728 | tf_op jit(solution)/shard_map/all_to_all | solution.py:438
  10.6 2.3 %copy-done.2 = bf16[768,3072]{1,0:T(8,128)(2,1)S(1)} copy-done((bf16[768,3072]{1,0:T(8,128)(2,1)S(1)}, bf16[768,3072]{1,0:T(8,128)(2,1)}, u32[]{:S(2)}) %copy-start.2) | copy-done | bytes 4718616
  16.0 6.5 %collective-permute-start.3 = (f32[2,2,3072]{2,1,0:T(2,128)S(1)}, f32[2,2,3072]{2,1,0:T(2,128)S(1)}, u32[]{:S(2)}, u32[]{:S(2)}) collective-permute-start(f32[2,2,3072]{2,1,0:T(2,128)S(1)} %pad_maximum_fusion.3.refs_0_), channel_id=1, source_target_pairs={{0,96},{16,176},{32,128},{48,208},{64,160},{80,240},{96,192},{112,... | collective-permute-start | bytes 147464 | tf_op jit(solution)/shard_map/ppermute | solution.py:32
  23.3 4.5 %collective-permute-start.4 = (f32[2,3072]{1,0:T(2,128)S(1)}, f32[2,3072]{1,0:T(2,128)S(1)}, u32[]{:S(2)}, u32[]{:S(2)}) collective-permute-start(f32[2,3072]{1,0:T(2,128)S(1)} %shard_map.74), channel_id=1, source_target_pairs={{0,128},{16,144},{32,160},{48,176},{64,192},{80,208},{96,224},{112... | collective-permute-start | bytes 73736 | tf_op jit(solution)/shard_map/ppermute | solution.py:32
  27.8 2.4 %collective-permute-done.4 = f32[2,3072]{1,0:T(2,128)S(1)} collective-permute-done((f32[2,3072]{1,0:T(2,128)S(1)}, f32[2,3072]{1,0:T(2,128)S(1)}, u32[]{:S(2)}, u32[]{:S(2)}) %collective-permute-start.4) | collective-permute-done | bytes 24608 | tf_op jit(solution)/shard_map/ppermute | solution.py:32
  30.3 3.3 %collective-permute-start.5 = (f32[7,2,3072]{2,1,0:T(2,128)S(1)}, f32[7,2,3072]{2,1,0:T(2,128)S(1)}, u32[]{:S(2)}, u32[]{:S(2)}) collective-permute-start(f32[7,2,3072]{2,1,0:T(2,128)S(1)} %pad_maximum_fusion.2.refs_1_), channel_id=1, source_target_pairs={{0,16},{16,0},{1,17},{17,1},{2,18},{18,2},{3,19},{19,3},{4,20},{20... | collective-permute-start | bytes 516104 | tf_op jit(solution)/shard_map/ppermute | solution.py:24
  34.6 2.3 %copy-done.3 = bf16[768,3072]{1,0:T(8,128)(2,1)S(1)} copy-done((bf16[768,3072]{1,0:T(8,128)(2,1)S(1)}, bf16[768,3072]{1,0:T(8,128)(2,1)}, u32[]{:S(2)}) %copy-start.3) | copy-done | bytes 4718616
  37.0 3.6 %shard_map.75 = (bf16[192,3200]{1,0:T(8,128)(2,1)S(1)}, bf16[192,3200]{1,0:T(8,128)(2,1)S(1)}) custom-call(s32[2]{0:T(128)S(1)} %pad_add_fusion.place.refs_0_, bf16[16,8,8,768]{3,2,1,0:T(8,128)(2,1)S(1)} %all-to-all-done.gathered, f32[1,768]{1,0:T(1,128)S(1)} %reshape.19.gain, bf16[768,3072]{1,0:T(8,128)(2,1)S(1)} %copy-done.3, ...), custom_call_target="tpu_custom_call" | custom-call | flops 1811939328 | bytes 7667712 | tf_op jit(solution)/shard_map/pallas_call | solution.py:167
  42.0 5.2 %shard_map.76 = (bf16[256,3200]{1,0:T(8,128)(2,1)S(1)}, bf16[384,3200]{1,0:T(8,128)(2,1)S(1)}) custom-call(s32[2]{0:T(128)S(1)} %pad_add_fusion.place.refs_0_, bf16[16,8,8,768]{3,2,1,0:T(8,128)(2,1)S(1)} %all-to-all-done.gathered, f32[1,768]{1,0:T(1,128)S(1)} %reshape.19.gain, bf16[768,3072]{1,0:T(8,128)(2,1)S(1)} %copy-done.3, ...), custom_call_target="tpu_custom_call" | custom-call | flops 3019898880 | bytes 9633792 | tf_op jit(solution)/shard_map/pallas_call | solution.py:167
  47.4 5.7 %collective-permute-start.8 = (bf16[32,3200]{1,0:T(8,128)(2,1)S(1)}, bf16[32,3200]{1,0:T(8,128)(2,1)S(1)}, u32[]{:S(2)}, u32[]{:S(2)}) collective-permute-start(bf16[32,3200]{1,0:T(8,128)(2,1)S(1)} %shard_map.77), channel_id=1, source_target_pairs={{0,32},{16,240},{32,64},{48,16},{64,96},{80,48},{96,128},{112,80},... | collective-permute-start | bytes 614408 | tf_op jit(solution)/shard_map/ppermute | solution.py:32
  55.9 3.2 %collective-permute-start.9 = (bf16[64,3200]{1,0:T(8,128)(2,1)S(1)}, bf16[64,3200]{1,0:T(8,128)(2,1)S(1)}, u32[]{:S(2)}, u32[]{:S(2)}) collective-permute-start(bf16[64,3200]{1,0:T(8,128)(2,1)S(1)} %shard_map.78), channel_id=1, source_target_pairs={{0,32},{16,240},{32,64},{48,16},{64,96},{80,48},{96,128},{112,80},... | collective-permute-start | bytes 1228808 | tf_op jit(solution)/shard_map/ppermute | solution.py:32
  59.3 2.0 %collective-permute-start.19 = (bf16[64,3200]{1,0:T(8,128)(2,1)S(1)}, bf16[64,3200]{1,0:T(8,128)(2,1)S(1)}, u32[]{:S(2)}, u32[]{:S(2)}) collective-permute-start(bf16[64,3200]{1,0:T(8,128)(2,1)S(1)} %shard_map.84), channel_id=1, source_target_pairs={{0,32},{16,240},{32,64},{48,16},{64,96},{80,48},{96,128},{112,80},... | collective-permute-start | bytes 1228808 | tf_op jit(solution)/shard_map/ppermute | solution.py:32
  61.3 2.7 %collective-permute-done.9.moving = bf16[64,3200]{1,0:T(8,128)(2,1)S(1)} collective-permute-done((bf16[64,3200]{1,0:T(8,128)(2,1)S(1)}, bf16[64,3200]{1,0:T(8,128)(2,1)S(1)}, u32[]{:S(2)}, u32[]{:S(2)}) %collective-permute-start.9) | collective-permute-done | bytes 409632 | tf_op jit(solution)/shard_map/ppermute | solution.py:32
  64.2 3.4 %collective-permute-start.10 = (bf16[64,3200]{1,0:T(8,128)(2,1)S(1)}, bf16[64,3200]{1,0:T(8,128)(2,1)S(1)}, u32[]{:S(2)}, u32[]{:S(2)}) collective-permute-start(bf16[64,3200]{1,0:T(8,128)(2,1)S(1)} %shard_map.79), channel_id=1, source_target_pairs={{0,32},{16,240},{32,64},{48,16},{64,96},{80,48},{96,128},{112,80},... | collective-permute-start | bytes 1228808 | tf_op jit(solution)/shard_map/ppermute | solution.py:32
  68.6 3.2 %collective-permute-start.20 = (bf16[64,3200]{1,0:T(8,128)(2,1)S(1)}, bf16[64,3200]{1,0:T(8,128)(2,1)S(1)}, u32[]{:S(2)}, u32[]{:S(2)}) collective-permute-start(bf16[64,3200]{1,0:T(8,128)(2,1)S(1)} %shard_map.85), channel_id=1, source_target_pairs={{0,32},{16,240},{32,64},{48,16},{64,96},{80,48},{96,128},{112,80},... | collective-permute-start | bytes 1228808 | tf_op jit(solution)/shard_map/ppermute | solution.py:32
  73.0 3.2 %collective-permute-start.11 = (bf16[64,3200]{1,0:T(8,128)(2,1)S(1)}, bf16[64,3200]{1,0:T(8,128)(2,1)S(1)}, u32[]{:S(2)}, u32[]{:S(2)}) collective-permute-start(bf16[64,3200]{1,0:T(8,128)(2,1)S(1)} %shard_map.80), channel_id=1, source_target_pairs={{0,32},{16,240},{32,64},{48,16},{64,96},{80,48},{96,128},{112,80},... | collective-permute-start | bytes 1228808 | tf_op jit(solution)/shard_map/ppermute | solution.py:32
  77.4 3.2 %collective-permute-start.21 = (bf16[64,3200]{1,0:T(8,128)(2,1)S(1)}, bf16[64,3200]{1,0:T(8,128)(2,1)S(1)}, u32[]{:S(2)}, u32[]{:S(2)}) collective-permute-start(bf16[64,3200]{1,0:T(8,128)(2,1)S(1)} %shard_map.86), channel_id=1, source_target_pairs={{0,32},{16,240},{32,64},{48,16},{64,96},{80,48},{96,128},{112,80},... | collective-permute-start | bytes 1228808 | tf_op jit(solution)/shard_map/ppermute | solution.py:32
  81.7 4.5 %collective-permute-start.12 = (bf16[32,3200]{1,0:T(8,128)(2,1)S(1)}, bf16[32,3200]{1,0:T(8,128)(2,1)S(1)}, u32[]{:S(2)}, u32[]{:S(2)}) collective-permute-start(bf16[32,3200]{1,0:T(8,128)(2,1)S(1)} %shard_map.81), channel_id=1, source_target_pairs={{0,16},{16,0},{1,17},{17,1},{2,18},{18,2},{3,19},{19,3},{4,20},{20... | collective-permute-start | bytes 614408 | tf_op jit(solution)/shard_map/ppermute | solution.py:24
  86.2 4.3 %collective-permute-start.22 = (bf16[32,3200]{1,0:T(8,128)(2,1)S(1)}, bf16[32,3200]{1,0:T(8,128)(2,1)S(1)}, u32[]{:S(2)}, u32[]{:S(2)}) collective-permute-start(bf16[32,3200]{1,0:T(8,128)(2,1)S(1)} %shard_map.87), channel_id=1, source_target_pairs={{0,16},{16,0},{1,17},{17,1},{2,18},{18,2},{3,19},{19,3},{4,20},{20... | collective-permute-start | bytes 614408 | tf_op jit(solution)/shard_map/ppermute | solution.py:24
  95.7 5.8 %collective-permute-done.14.refs_3_ = bf16[64,3072]{1,0:T(8,128)(2,1)S(1)} collective-permute-done((bf16[64,3072]{1,0:T(8,128)(2,1)S(1)}, bf16[64,3072]{1,0:T(8,128)(2,1)S(1)}, u32[]{:S(2)}, u32[]{:S(2)}) %collective-permute-start.14) | collective-permute-done | bytes 393248 | tf_op jit(solution)/shard_map/ppermute | solution.py:32
  102.4 3.3 %collective-permute-done.24.refs_8_ = bf16[64,3072]{1,0:T(8,128)(2,1)S(1)} collective-permute-done((bf16[64,3072]{1,0:T(8,128)(2,1)S(1)}, bf16[64,3072]{1,0:T(8,128)(2,1)S(1)}, u32[]{:S(2)}, u32[]{:S(2)}) %collective-permute-start.24) | collective-permute-done | bytes 393248 | tf_op jit(solution)/shard_map/ppermute | solution.py:32
  107.8 2.1 %collective-permute-done.15.refs_4_ = bf16[64,3072]{1,0:T(8,128)(2,1)S(1)} collective-permute-done((bf16[64,3072]{1,0:T(8,128)(2,1)S(1)}, bf16[64,3072]{1,0:T(8,128)(2,1)S(1)}, u32[]{:S(2)}, u32[]{:S(2)}) %collective-permute-start.15) | collective-permute-done | bytes 393248 | tf_op jit(solution)/shard_map/ppermute | solution.py:32
  109.9 2.7 %collective-permute-start.17 = (bf16[64,3072]{1,0:T(8,128)(2,1)S(1)}, bf16[64,3072]{1,0:T(8,128)(2,1)S(1)}, u32[]{:S(2)}, u32[]{:S(2)}) collective-permute-start(bf16[64,3072]{1,0:T(8,128)(2,1)S(1)} %collective-permute-done.15.refs_4_), channel_id=1, source_target_pairs={{0,16},{16,0},{1,17},{17,1},{2,18},{18,2},{3,19},{19,3},{4,20},{20... | collective-permute-start | bytes 1179656 | tf_op jit(solution)/shard_map/ppermute | solution.py:24
  114.2 2.7 %collective-permute-start.27 = (bf16[64,3072]{1,0:T(8,128)(2,1)S(1)}, bf16[64,3072]{1,0:T(8,128)(2,1)S(1)}, u32[]{:S(2)}, u32[]{:S(2)}) collective-permute-start(bf16[64,3072]{1,0:T(8,128)(2,1)S(1)} %collective-permute-done.25.refs_9_), channel_id=1, source_target_pairs={{0,16},{16,0},{1,17},{17,1},{2,18},{18,2},{3,19},{19,3},{4,20},{20... | collective-permute-start | bytes 1179656 | tf_op jit(solution)/shard_map/ppermute | solution.py:24
  118.2 5.3 %shard_map.90.refs_0_ = bf16[16,5,8,768]{3,2,1,0:T(8,128)(2,1)} custom-call(s32[2]{0:T(128)S(1)} %pad_add_fusion.place.refs_0_, bf16[3072,768]{1,0:T(8,128)(2,1)S(1)} %bitcast.9, bf16[64,3072]{1,0:T(8,128)(2,1)S(1)} %pad_maximum_fusion.refs_2_, bf16[64,3072]{1,0:T(8,128)(2,1)S(1)} %collective-permute-done.14.refs_3_, ...), custom_call_target="tpu_custom_call" | custom-call | flops 3019898880 | bytes 9633792 | tf_op jit(solution)/shard_map/pallas_call | solution.py:380
  123.5 3.6 %all-to-all-start.1 = ((bf16[16,5,8,768]{3,2,1,0:T(8,128)(2,1)}), bf16[16,5,8,768]{3,2,1,0:T(8,128)(2,1)S(1)}, u32[]{:S(2)}, u32[]{:S(2)}) async-start(bf16[16,5,8,768]{3,2,1,0:T(8,128)(2,1)} %shard_map.90.refs_0_), calls=%async_computation.1 | async-start | bytes 1966080 | tf_op jit(solution)/shard_map/all_to_all | solution.py:438
  128.1 2.1 %collective-permute-start.31 = (bf16[64,3072]{1,0:T(8,128)(2,1)S(1)}, bf16[64,3072]{1,0:T(8,128)(2,1)S(1)}, u32[]{:S(2)}, u32[]{:S(2)}) collective-permute-start(bf16[64,3072]{1,0:T(8,128)(2,1)S(1)} %collective-permute-done.30.refs_2_.value), channel_id=1, source_target_pairs={{0,16},{16,0},{1,17},{17,1},{2,18},{18,2},{3,19},{19,3},{4,20},{20... | collective-permute-start | bytes 1179656 | tf_op jit(solution)/shard_map/ppermute | solution.py:24
  131.9 2.3 %copy-done = bf16[3072,768]{1,0:T(8,128)(2,1)S(1)} copy-done((bf16[3072,768]{1,0:T(8,128)(2,1)S(1)}, bf16[3072,768]{1,0:T(8,128)(2,1)}, u32[]{:S(2)}) %copy-start) | copy-done | bytes 4718616
  137.3 2.1 %collective-permute-start.35 = (bf16[32,3072]{1,0:T(8,128)(2,1)S(1)}, bf16[32,3072]{1,0:T(8,128)(2,1)S(1)}, u32[]{:S(2)}, u32[]{:S(2)}) collective-permute-start(bf16[32,3072]{1,0:T(8,128)(2,1)S(1)} %shard_map.95.refs_5_), channel_id=1, source_target_pairs={{0,16},{16,0},{1,17},{17,1},{2,18},{18,2},{3,19},{19,3},{4,20},{20... | collective-permute-start | bytes 589832 | tf_op jit(solution)/shard_map/ppermute | solution.py:24
  140.4 2.3 %copy-done.1 = bf16[3072,768]{1,0:T(8,128)(2,1)S(1)} copy-done((bf16[3072,768]{1,0:T(8,128)(2,1)S(1)}, bf16[3072,768]{1,0:T(8,128)(2,1)}, u32[]{:S(2)}) %copy-start.1) | copy-done | bytes 4718616
  144.5 16.2 %all_to_all.15.far = bf16[16,3,8,768]{3,2,1,0:T(8,128)(2,1)S(1)} all-to-all(bf16[16,3,8,768]{3,2,1,0:T(8,128)(2,1)S(1)} %shard_map.96), channel_id=1, replica_groups=mesh['z'=8,'core'=2,'y'=4,'x'=4] {'y','x'}, dimensions={0} | all-to-all | bytes 1179648 | tf_op jit(solution)/shard_map/all_to_all | solution.py:438
  160.7 2.0 %shard_map.97 = bf16[8,8,768]{2,1,0:T(8,128)(2,1)} custom-call(s32[2]{0:T(128)S(1)} %pad_add_fusion.place.refs_0_, bf16[16,5,8,768]{3,2,1,0:T(8,128)(2,1)S(1)} %all-to-all-done.1.near, bf16[16,3,8,768]{3,2,1,0:T(8,128)(2,1)S(1)} %all_to_all.15.far, f32[8,8,768]{2,1,0:T(8,128)S(1)} %shard_map.89.refs_12_.base), custom_call_target="tpu_custom_call" | custom-call | tf_op jit(solution)/shard_map/pallas_call | solution.py:420
  (103 shorter events, 36.5 us)
Async XLA Ops:
  2.8 31.8 %all-to-all-start = ((bf16[16,8,8,768]{3,2,1,0:T(8,128)(2,1)}), bf16[16,8,8,768]{3,2,1,0:T(8,128)(2,1)S(1)}, u32[]{:S(2)}, u32[]{:S(2)}) async-start(bf16[16,8,8,768]{3,2,1,0:T(8,128)(2,1)} %shard_map.73.refs_0_), calls=%async_computation | async-start | bytes 3145728 | tf_op jit(solution)/shard_map/all_to_all | solution.py:438
  16.0 14.2 %collective-permute-start.3 = (f32[2,2,3072]{2,1,0:T(2,128)S(1)}, f32[2,2,3072]{2,1,0:T(2,128)S(1)}, u32[]{:S(2)}, u32[]{:S(2)}) collective-permute-start(f32[2,2,3072]{2,1,0:T(2,128)S(1)} %pad_maximum_fusion.3.refs_0_), channel_id=1, source_target_pairs={{0,96},{16,176},{32,128},{48,208},{64,160},{80,240},{96,192},{112,... | collective-permute-start | bytes 147464 | tf_op jit(solution)/shard_map/ppermute | solution.py:32
  22.6 7.6 %collective-permute-start.2 = (f32[2,2,3072]{2,1,0:T(2,128)S(1)}, f32[2,2,3072]{2,1,0:T(2,128)S(1)}, u32[]{:S(2)}, u32[]{:S(2)}) collective-permute-start(f32[2,2,3072]{2,1,0:T(2,128)S(1)} %pad_maximum_fusion.3.refs_0_), channel_id=1, source_target_pairs={{0,64},{16,208},{32,96},{48,240},{64,128},{80,16},{96,160},{112,48... | collective-permute-start | bytes 147464 | tf_op jit(solution)/shard_map/ppermute | solution.py:32
  22.8 7.4 %collective-permute-start.1 = (f32[2,2,3072]{2,1,0:T(2,128)S(1)}, f32[2,2,3072]{2,1,0:T(2,128)S(1)}, u32[]{:S(2)}, u32[]{:S(2)}) collective-permute-start(f32[2,2,3072]{2,1,0:T(2,128)S(1)} %pad_maximum_fusion.3.refs_0_), channel_id=1, source_target_pairs={{0,32},{16,240},{32,64},{48,16},{64,96},{80,48},{96,128},{112,80},... | collective-permute-start | bytes 147464 | tf_op jit(solution)/shard_map/ppermute | solution.py:32
  23.3 6.9 %collective-permute-start.4 = (f32[2,3072]{1,0:T(2,128)S(1)}, f32[2,3072]{1,0:T(2,128)S(1)}, u32[]{:S(2)}, u32[]{:S(2)}) collective-permute-start(f32[2,3072]{1,0:T(2,128)S(1)} %shard_map.74), channel_id=1, source_target_pairs={{0,128},{16,144},{32,160},{48,176},{64,192},{80,208},{96,224},{112... | collective-permute-start | bytes 73736 | tf_op jit(solution)/shard_map/ppermute | solution.py:32
  30.3 4.3 %collective-permute-start.5 = (f32[7,2,3072]{2,1,0:T(2,128)S(1)}, f32[7,2,3072]{2,1,0:T(2,128)S(1)}, u32[]{:S(2)}, u32[]{:S(2)}) collective-permute-start(f32[7,2,3072]{2,1,0:T(2,128)S(1)} %pad_maximum_fusion.2.refs_1_), channel_id=1, source_target_pairs={{0,16},{16,0},{1,17},{17,1},{2,18},{18,2},{3,19},{19,3},{4,20},{20... | collective-permute-start | bytes 516104 | tf_op jit(solution)/shard_map/ppermute | solution.py:24
  40.6 6.7 %collective-permute-start.7 = (bf16[192,3200]{1,0:T(8,128)(2,1)S(1)}, bf16[192,3200]{1,0:T(8,128)(2,1)S(1)}, u32[]{:S(2)}, u32[]{:S(2)}) collective-permute-start(bf16[192,3200]{1,0:T(8,128)(2,1)S(1)} %get-tuple-element.9.refs_0_), channel_id=1, source_target_pairs={{0,16},{16,0},{1,17},{17,1},{2,18},{18,2},{3,19},{19,3},{4,20},{20... | collective-permute-start | bytes 3686408 | tf_op jit(solution)/shard_map/ppermute | solution.py:24
  47.2 14.1 %collective-permute-start.6 = (bf16[256,3200]{1,0:T(8,128)(2,1)S(1)}, bf16[256,3200]{1,0:T(8,128)(2,1)S(1)}, u32[]{:S(2)}, u32[]{:S(2)}) collective-permute-start(bf16[256,3200]{1,0:T(8,128)(2,1)S(1)} %get-tuple-element.11), channel_id=1, source_target_pairs={{0,16},{16,0},{1,17},{17,1},{2,18},{18,2},{3,19},{19,3},{4,20},{20... | collective-permute-start | bytes 4915208 | tf_op jit(solution)/shard_map/ppermute | solution.py:24
  47.4 8.4 %collective-permute-start.8 = (bf16[32,3200]{1,0:T(8,128)(2,1)S(1)}, bf16[32,3200]{1,0:T(8,128)(2,1)S(1)}, u32[]{:S(2)}, u32[]{:S(2)}) collective-permute-start(bf16[32,3200]{1,0:T(8,128)(2,1)S(1)} %shard_map.77), channel_id=1, source_target_pairs={{0,32},{16,240},{32,64},{48,16},{64,96},{80,48},{96,128},{112,80},... | collective-permute-start | bytes 614408 | tf_op jit(solution)/shard_map/ppermute | solution.py:32
  53.1 6.0 %collective-permute-start.18 = (bf16[32,3200]{1,0:T(8,128)(2,1)S(1)}, bf16[32,3200]{1,0:T(8,128)(2,1)S(1)}, u32[]{:S(2)}, u32[]{:S(2)}) collective-permute-start(bf16[32,3200]{1,0:T(8,128)(2,1)S(1)} %shard_map.83), channel_id=1, source_target_pairs={{0,32},{16,240},{32,64},{48,16},{64,96},{80,48},{96,128},{112,80},... | collective-permute-start | bytes 614408 | tf_op jit(solution)/shard_map/ppermute | solution.py:32
  55.9 8.1 %collective-permute-start.9 = (bf16[64,3200]{1,0:T(8,128)(2,1)S(1)}, bf16[64,3200]{1,0:T(8,128)(2,1)S(1)}, u32[]{:S(2)}, u32[]{:S(2)}) collective-permute-start(bf16[64,3200]{1,0:T(8,128)(2,1)S(1)} %shard_map.78), channel_id=1, source_target_pairs={{0,32},{16,240},{32,64},{48,16},{64,96},{80,48},{96,128},{112,80},... | collective-permute-start | bytes 1228808 | tf_op jit(solution)/shard_map/ppermute | solution.py:32
  59.3 9.1 %collective-permute-start.19 = (bf16[64,3200]{1,0:T(8,128)(2,1)S(1)}, bf16[64,3200]{1,0:T(8,128)(2,1)S(1)}, u32[]{:S(2)}, u32[]{:S(2)}) collective-permute-start(bf16[64,3200]{1,0:T(8,128)(2,1)S(1)} %shard_map.84), channel_id=1, source_target_pairs={{0,32},{16,240},{32,64},{48,16},{64,96},{80,48},{96,128},{112,80},... | collective-permute-start | bytes 1228808 | tf_op jit(solution)/shard_map/ppermute | solution.py:32
  64.2 8.6 %collective-permute-start.10 = (bf16[64,3200]{1,0:T(8,128)(2,1)S(1)}, bf16[64,3200]{1,0:T(8,128)(2,1)S(1)}, u32[]{:S(2)}, u32[]{:S(2)}) collective-permute-start(bf16[64,3200]{1,0:T(8,128)(2,1)S(1)} %shard_map.79), channel_id=1, source_target_pairs={{0,32},{16,240},{32,64},{48,16},{64,96},{80,48},{96,128},{112,80},... | collective-permute-start | bytes 1228808 | tf_op jit(solution)/shard_map/ppermute | solution.py:32
  68.6 8.6 %collective-permute-start.20 = (bf16[64,3200]{1,0:T(8,128)(2,1)S(1)}, bf16[64,3200]{1,0:T(8,128)(2,1)S(1)}, u32[]{:S(2)}, u32[]{:S(2)}) collective-permute-start(bf16[64,3200]{1,0:T(8,128)(2,1)S(1)} %shard_map.85), channel_id=1, source_target_pairs={{0,32},{16,240},{32,64},{48,16},{64,96},{80,48},{96,128},{112,80},... | collective-permute-start | bytes 1228808 | tf_op jit(solution)/shard_map/ppermute | solution.py:32
  73.0 8.6 %collective-permute-start.11 = (bf16[64,3200]{1,0:T(8,128)(2,1)S(1)}, bf16[64,3200]{1,0:T(8,128)(2,1)S(1)}, u32[]{:S(2)}, u32[]{:S(2)}) collective-permute-start(bf16[64,3200]{1,0:T(8,128)(2,1)S(1)} %shard_map.80), channel_id=1, source_target_pairs={{0,32},{16,240},{32,64},{48,16},{64,96},{80,48},{96,128},{112,80},... | collective-permute-start | bytes 1228808 | tf_op jit(solution)/shard_map/ppermute | solution.py:32
  77.4 8.8 %collective-permute-start.21 = (bf16[64,3200]{1,0:T(8,128)(2,1)S(1)}, bf16[64,3200]{1,0:T(8,128)(2,1)S(1)}, u32[]{:S(2)}, u32[]{:S(2)}) collective-permute-start(bf16[64,3200]{1,0:T(8,128)(2,1)S(1)} %shard_map.86), channel_id=1, source_target_pairs={{0,32},{16,240},{32,64},{48,16},{64,96},{80,48},{96,128},{112,80},... | collective-permute-start | bytes 1228808 | tf_op jit(solution)/shard_map/ppermute | solution.py:32
  81.7 8.9 %collective-permute-start.12 = (bf16[32,3200]{1,0:T(8,128)(2,1)S(1)}, bf16[32,3200]{1,0:T(8,128)(2,1)S(1)}, u32[]{:S(2)}, u32[]{:S(2)}) collective-permute-start(bf16[32,3200]{1,0:T(8,128)(2,1)S(1)} %shard_map.81), channel_id=1, source_target_pairs={{0,16},{16,0},{1,17},{17,1},{2,18},{18,2},{3,19},{19,3},{4,20},{20... | collective-permute-start | bytes 614408 | tf_op jit(solution)/shard_map/ppermute | solution.py:24
  86.2 6.1 %collective-permute-start.22 = (bf16[32,3200]{1,0:T(8,128)(2,1)S(1)}, bf16[32,3200]{1,0:T(8,128)(2,1)S(1)}, u32[]{:S(2)}, u32[]{:S(2)}) collective-permute-start(bf16[32,3200]{1,0:T(8,128)(2,1)S(1)} %shard_map.87), channel_id=1, source_target_pairs={{0,16},{16,0},{1,17},{17,1},{2,18},{18,2},{3,19},{19,3},{4,20},{20... | collective-permute-start | bytes 614408 | tf_op jit(solution)/shard_map/ppermute | solution.py:24
  94.5 7.0 %collective-permute-start.14 = (bf16[64,3072]{1,0:T(8,128)(2,1)S(1)}, bf16[64,3072]{1,0:T(8,128)(2,1)S(1)}, u32[]{:S(2)}, u32[]{:S(2)}) collective-permute-start(bf16[64,3072]{1,0:T(8,128)(2,1)S(1)} %pad_maximum_fusion.refs_2_), channel_id=1, source_target_pairs={{0,32},{16,240},{32,64},{48,16},{64,96},{80,48},{96,128},{112,80},... | collective-permute-start | bytes 1179656 | tf_op jit(solution)/shard_map/ppermute | solution.py:32
  95.6 10.1 %collective-permute-start.24 = (bf16[64,3072]{1,0:T(8,128)(2,1)S(1)}, bf16[64,3072]{1,0:T(8,128)(2,1)S(1)}, u32[]{:S(2)}, u32[]{:S(2)}) collective-permute-start(bf16[64,3072]{1,0:T(8,128)(2,1)S(1)} %pad_maximum_fusion.1.refs_7_), channel_id=1, source_target_pairs={{0,32},{16,240},{32,64},{48,16},{64,96},{80,48},{96,128},{112,80},... | collective-permute-start | bytes 1179656 | tf_op jit(solution)/shard_map/ppermute | solution.py:32
  101.5 8.4 %collective-permute-start.15 = (bf16[64,3072]{1,0:T(8,128)(2,1)S(1)}, bf16[64,3072]{1,0:T(8,128)(2,1)S(1)}, u32[]{:S(2)}, u32[]{:S(2)}) collective-permute-start(bf16[64,3072]{1,0:T(8,128)(2,1)S(1)} %collective-permute-done.14.refs_3_), channel_id=1, source_target_pairs={{0,32},{16,240},{32,64},{48,16},{64,96},{80,48},{96,128},{112,80},... | collective-permute-start | bytes 1179656 | tf_op jit(solution)/shard_map/ppermute | solution.py:32
  105.7 8.4 %collective-permute-start.25 = (bf16[64,3072]{1,0:T(8,128)(2,1)S(1)}, bf16[64,3072]{1,0:T(8,128)(2,1)S(1)}, u32[]{:S(2)}, u32[]{:S(2)}) collective-permute-start(bf16[64,3072]{1,0:T(8,128)(2,1)S(1)} %collective-permute-done.24.refs_8_), channel_id=1, source_target_pairs={{0,32},{16,240},{32,64},{48,16},{64,96},{80,48},{96,128},{112,80},... | collective-permute-start | bytes 1179656 | tf_op jit(solution)/shard_map/ppermute | solution.py:32
  106.6 10.3 %collective-permute-start.16 = (bf16[64,3072]{1,0:T(8,128)(2,1)S(1)}, bf16[64,3072]{1,0:T(8,128)(2,1)S(1)}, u32[]{:S(2)}, u32[]{:S(2)}) collective-permute-start(bf16[64,3072]{1,0:T(8,128)(2,1)S(1)} %collective-permute-done.14.refs_3_), channel_id=1, source_target_pairs={{0,16},{16,0},{1,17},{17,1},{2,18},{18,2},{3,19},{19,3},{4,20},{20... | collective-permute-start | bytes 1179656 | tf_op jit(solution)/shard_map/ppermute | solution.py:24
  107.8 9.4 %collective-permute-start.26 = (bf16[64,3072]{1,0:T(8,128)(2,1)S(1)}, bf16[64,3072]{1,0:T(8,128)(2,1)S(1)}, u32[]{:S(2)}, u32[]{:S(2)}) collective-permute-start(bf16[64,3072]{1,0:T(8,128)(2,1)S(1)} %collective-permute-done.24.refs_8_), channel_id=1, source_target_pairs={{0,16},{16,0},{1,17},{17,1},{2,18},{18,2},{3,19},{19,3},{4,20},{20... | collective-permute-start | bytes 1179656 | tf_op jit(solution)/shard_map/ppermute | solution.py:24
  109.9 7.3 %collective-permute-start.17 = (bf16[64,3072]{1,0:T(8,128)(2,1)S(1)}, bf16[64,3072]{1,0:T(8,128)(2,1)S(1)}, u32[]{:S(2)}, u32[]{:S(2)}) collective-permute-start(bf16[64,3072]{1,0:T(8,128)(2,1)S(1)} %collective-permute-done.15.refs_4_), channel_id=1, source_target_pairs={{0,16},{16,0},{1,17},{17,1},{2,18},{18,2},{3,19},{19,3},{4,20},{20... | collective-permute-start | bytes 1179656 | tf_op jit(solution)/shard_map/ppermute | solution.py:24
  114.2 4.0 %collective-permute-start.27 = (bf16[64,3072]{1,0:T(8,128)(2,1)S(1)}, bf16[64,3072]{1,0:T(8,128)(2,1)S(1)}, u32[]{:S(2)}, u32[]{:S(2)}) collective-permute-start(bf16[64,3072]{1,0:T(8,128)(2,1)S(1)} %collective-permute-done.25.refs_9_), channel_id=1, source_target_pairs={{0,16},{16,0},{1,17},{17,1},{2,18},{18,2},{3,19},{19,3},{4,20},{20... | collective-permute-start | bytes 1179656 | tf_op jit(solution)/shard_map/ppermute | solution.py:24
  116.9 10.3 %collective-permute-start.28 = (bf16[64,3072]{1,0:T(8,128)(2,1)S(1)}, bf16[64,3072]{1,0:T(8,128)(2,1)S(1)}, u32[]{:S(2)}, u32[]{:S(2)}) collective-permute-start(bf16[64,3072]{1,0:T(8,128)(2,1)S(1)} %collective-permute-done.15.refs_4_), channel_id=1, source_target_pairs={{0,32},{16,240},{32,64},{48,16},{64,96},{80,48},{96,128},{112,80},... | collective-permute-start | bytes 1179656 | tf_op jit(solution)/shard_map/ppermute | solution.py:32
  117.0 11.1 %collective-permute-start.30 = (bf16[64,3072]{1,0:T(8,128)(2,1)S(1)}, bf16[64,3072]{1,0:T(8,128)(2,1)S(1)}, u32[]{:S(2)}, u32[]{:S(2)}) collective-permute-start(bf16[64,3072]{1,0:T(8,128)(2,1)S(1)} %collective-permute-done.25.refs_9_), channel_id=1, source_target_pairs={{0,32},{16,240},{32,64},{48,16},{64,96},{80,48},{96,128},{112,80},... | collective-permute-start | bytes 1179656 | tf_op jit(solution)/shard_map/ppermute | solution.py:32
  123.5 21.0 %all-to-all-start.1 = ((bf16[16,5,8,768]{3,2,1,0:T(8,128)(2,1)}), bf16[16,5,8,768]{3,2,1,0:T(8,128)(2,1)S(1)}, u32[]{:S(2)}, u32[]{:S(2)}) async-start(bf16[16,5,8,768]{3,2,1,0:T(8,128)(2,1)} %shard_map.90.refs_0_), calls=%async_computation.1 | async-start | bytes 1966080 | tf_op jit(solution)/shard_map/all_to_all | solution.py:438
  127.2 4.7 %collective-permute-start.29 = (bf16[64,3072]{1,0:T(8,128)(2,1)S(1)}, bf16[64,3072]{1,0:T(8,128)(2,1)S(1)}, u32[]{:S(2)}, u32[]{:S(2)}) collective-permute-start(bf16[64,3072]{1,0:T(8,128)(2,1)S(1)} %collective-permute-done.28.refs_0_.value), channel_id=1, source_target_pairs={{0,16},{16,0},{1,17},{17,1},{2,18},{18,2},{3,19},{19,3},{4,20},{20... | collective-permute-start | bytes 1179656 | tf_op jit(solution)/shard_map/ppermute | solution.py:24
  130.2 5.5 %collective-permute-start.32 = (bf16[32,3072]{1,0:T(8,128)(2,1)S(1)}, bf16[32,3072]{1,0:T(8,128)(2,1)S(1)}, u32[]{:S(2)}, u32[]{:S(2)}) collective-permute-start(bf16[32,3072]{1,0:T(8,128)(2,1)S(1)} %shard_map.92), channel_id=1, source_target_pairs={{0,32},{16,240},{32,64},{48,16},{64,96},{80,48},{96,128},{112,80},... | collective-permute-start | bytes 589832 | tf_op jit(solution)/shard_map/ppermute | solution.py:32
  130.3 7.0 %collective-permute-start.34 = (bf16[32,3072]{1,0:T(8,128)(2,1)S(1)}, bf16[32,3072]{1,0:T(8,128)(2,1)S(1)}, u32[]{:S(2)}, u32[]{:S(2)}) collective-permute-start(bf16[32,3072]{1,0:T(8,128)(2,1)S(1)} %shard_map.94), channel_id=1, source_target_pairs={{0,32},{16,240},{32,64},{48,16},{64,96},{80,48},{96,128},{112,80},... | collective-permute-start | bytes 589832 | tf_op jit(solution)/shard_map/ppermute | solution.py:32
  (18 other events, 158.3 us)
where the time goes:
time: 163 us
  starting transfers between devices  79.9 us (49%)
  waiting for transfers between devices  28.9 us (18%)
  Pallas kernels  26.9 us (17%)
  blocking collectives  16.2 us (10%)
  local copies, waits for them, and re-layouts  10.3 us (6%)
    ppermute x20, starting transfers between devices, onward(): return lax.ppermute(value, ('z', 'core'), pairs)  40.5 us
    ppermute x16, starting transfers between devices, swap(): return lax.ppermute(value, 'core', [(0, 1), (1, 0)])  28 us
    ppermute x20, waiting for transfers between devices, onward(): return lax.ppermute(value, ('z', 'core'), pairs)  24 us
    all_to_all x1, blocking collectives, exchange(): return lax.all_to_all(value, plane, 0, 0, tiled=True)  16.2 us
    all_to_all x2, starting transfers between devices, exchange(): return lax.all_to_all(value, plane, 0, 0, tiled=True)  11.4 us
    unnamed x24, local copies, waits for them, and re-layouts  10.3 us
    pallas_call x2, Pallas kernels, first_product(): pl.pallas_call(functools.partial(first_kernel, choose), in_specs=[scalars...  8.77 us
    pallas_call x2, Pallas kernels, merged_product(): pl.pallas_call(kernel, in_specs=[scalars] + [whole] * (len(done) + 1 + le...  7.12 us
  transfers between devices with their start and end apart: 38, of which 17 were waited for; matrix products, arithmetic and copies ran while one was open for 0% of the time, Pallas kernels for 12%

commit v1 on v0

--- a/solution.py
+++ b/solution.py
@@ -50,25 +50,6 @@
 
 def params(size):
     return pltpu.CompilerParams(vmem_limit_bytes=size * megabyte)
-
-
-def copies_kernel(offsets, place, tokens, *refs):
-    out = refs[-1]
-    for slot, steps in enumerate(offsets):
-        block = tokens[around(place[0], steps)]
-        for i in range(out.shape[0]):
-            out[i, slot] = block
-
-
-def copies(offsets, place, tokens, *before):
-    shape = (16, len(offsets)) + tokens.shape[1:]
-    return pl.pallas_call(
-        functools.partial(copies_kernel, offsets),
-        in_specs=[scalars, whole] + [anywhere] * len(before),
-        out_specs=whole,
-        out_shape=jax.ShapeDtypeStruct(shape, tokens.dtype),
-        compiler_params=params(16),
-    )(place, tokens, *before)
 
 
 def tops_kernel(gain, bias, weight, *refs):
@@ -105,20 +86,22 @@
 
 
 def early_blocks(core):
+    way = 1 - 2 * core
     theirs, ours = [], []
     for part in range(parts):
-        theirs += [(0, part, 1 - core), (2 - core, part, 1 - core), (2 - core, part, core)]
-        ours += [(0, part, core), (1 + core, part, core), (1 + core, part, 1 - core)]
+        theirs += [(4, part, 1 - core), (-3 * way, part, 1 - core), (-3 * way, part, core)]
+        ours += [(4, part, core), (3 * way, part, core), (3 * way, part, 1 - core)]
     return theirs, ours
 
 
 def later_blocks(core):
+    way = 1 - 2 * core
     theirs, ours = [], []
     for part in range(parts):
-        for first in (3, 5):
-            theirs += [(first + 1 - core, part, 1 - core), (first + 1 - core, part, core)]
-            ours += [(first + core, part, core), (first + core, part, 1 - core)]
-        ours += [(7, part, core), (7, part, 1 - core)]
+        for steps in (2, 1):
+            theirs += [(-steps * way, part, 1 - core), (-steps * way, part, core)]
+            ours += [(steps * way, part, core), (steps * way, part, 1 - core)]
+        ours += [(0, part, core), (0, part, 1 - core)]
     return theirs, ours
 
 
@@ -131,11 +114,11 @@
     lane = lax.broadcasted_iota(jnp.int32, (rows, 128), 1)
     kind = lax.div(lane, 16)
     here = lane - 16 * kind == 2 * z + core
-    for slot, (number, part, which) in enumerate(sum(choose(core), [])):
+    for slot, (steps, part, which) in enumerate(sum(choose(core), [])):
         span = slice(slot * rows, (slot + 1) * rows)
         base = 8 * part + 4 * which
         block = jnp.concatenate(
-            [gathered[base + i, number].astype(jnp.float32) for i in range(4)]
+            [gathered[base + i, around(z, steps)].astype(jnp.float32) for i in range(4)]
         )
         mean = jnp.sum(block, axis=1, keepdims=True) / features
         differ = block - mean
@@ -152,12 +135,12 @@
     theirs[:, -128:] = notes[:split]
     ours[:, -128:] = notes[split:]
 
-    def work(span):
+    step = 768
+    for first in range(0, weight.shape[1], step):
+        span = slice(first, first + step)
         value = jnp.dot(left[...], weight[:, span], preferred_element_type=jnp.float32)
         theirs[:, span] = value[:split].astype(jnp.bfloat16)
         ours[:, span] = value[split:].astype(jnp.bfloat16)
-
-    columns(weight.shape[1], 768, work)
 
 
 def first_product(choose, place, gathered, gain, weight, *before):
@@ -296,10 +279,11 @@
 
 
 def product_kernel(*refs):
-    tiles, weight, out = refs[:-2], refs[-2], refs[-1]
+    tiles, weight, out, held = refs[:-3], refs[-3], refs[-2], refs[-1]
     left = jnp.concatenate([tile[...] for tile in tiles])
     total = jnp.dot(left, weight[...], preferred_element_type=jnp.float32)
     out[...] = total.astype(jnp.bfloat16)
+    held[...] = weight[...]
 
 
 def merge_kernel(slots, earlier, place, *refs):
@@ -363,8 +347,11 @@
     return pl.pallas_call(
         product_kernel,
         in_specs=[whole] * (len(tiles) + 1),
-        out_specs=whole,
-        out_shape=jax.ShapeDtypeStruct((tokens, weight.shape[1]), jnp.bfloat16),
+        out_specs=[whole, whole],
+        out_shape=[
+            jax.ShapeDtypeStruct((tokens, weight.shape[1]), jnp.bfloat16),
+            jax.ShapeDtypeStruct(weight.shape, weight.dtype),
+        ],
         compiler_params=params(24),
         cost_estimate=second_cost(tokens, weight),
     )(*tiles, weight)
@@ -437,7 +424,7 @@
     def exchange(value):
         return lax.all_to_all(value, plane, 0, 0, tiled=True)
 
-    ready = copies((4, 3, -3, 2, -2, 1, -1, 0), place, grouped)
+    ready = jnp.broadcast_to(grouped[None], (16,) + grouped.shape)
     gathered = exchange(ready)
     mine = tops_product(norm_gain, norm_bias, weight_in, ready)
     pair = jnp.stack([mine, swap(mine)])
@@ -464,12 +451,13 @@
         step = onward(ring_sum(2, first, second, ours, theirs, step))
         step = onward(ring_sum(3, first + 2, second + 2, ours, theirs, step))
         other = swap(ring_sum(4, first + 5, 0, ours, theirs, step))
-        hidden.append(activate(features, first + 4, place, ours, step, other, tops, bias_in))
+        value = activate(features, first + 4, place, ours, step, other, tops, bias_in)
+        hidden.append(jnp.concatenate([value, swap(value)]))
 
     base = base_sum(grouped, bias_out)
     tiles, steps = [], []
     for part in range(parts):
-        step = jnp.concatenate([hidden[part], swap(hidden[part])])
+        step = hidden[part]
         own = [step]
         for _ in range(2):
             step = onward(step)
@@ -479,10 +467,12 @@
     near = merged_product(near_slots, 5, place, [], tiles, weight_out, base)
     four = [onward(passed(value, rows, near)) for value in steps]
     near = exchange(near)
-    done = second_product([value for step in steps for value in (step, swap(step))], weight_out)
+    done, held = second_product(
+        [value for step in steps for value in (step, swap(step))], weight_out
+    )
     four = [passed(value, rows, done) for value in four]
     far = [value for step in four for value in (step, swap(step))]
-    far = merged_product(far_slots, 3, place, [done], far, weight_out)
+    far = merged_product(far_slots, 3, place, [done], far, held)
     far = exchange(far)
     out = last_sum(place, near, far, base)
     return out.reshape(tokens.shape)

time: 163 us -> 159 us (0.975)
  Pallas kernels: 26.9 us -> 23.8 us
    unnamed x24 -> x20, local copies, waits for them, and re-layouts: 10.3 us -> 7.04 us
    broadcast_in_dim x0 -> x1, local copies, waits for them, and re-layouts: none -> 2.21 us  [body(): ready = jnp.broadcast_to(grouped[None], (16,) + grouped.shape)]
    pallas_call x1 -> x0, Pallas kernels: 1.87 us -> none  [copies(): pl.pallas_call(functools.partial(copies_kernel, offsets), in_specs=[scala...]
  transfers between devices with their start and end apart: 38 -> 38, of which waited for: 17 -> 18; matrix products, arithmetic and copies ran while one was open for 0% -> 0% of each run, Pallas kernels for 12% -> 12%
where the time goes in v1:
time: 159 us; the launch traced here: 158 us
  starting transfers between devices  79.3 us (50%)
  waiting for transfers between devices  30 us (19%)
  Pallas kernels  23.8 us (15%)
  blocking collectives  15.3 us (10%)
  local copies, waits for them, and re-layouts  9.26 us (6%)
    ppermute x20, starting transfers between devices, onward(): return lax.ppermute(value, ('z', 'core'), pairs)  40.3 us
    ppermute x16, starting transfers between devices, swap(): return lax.ppermute(value, 'core', [(0, 1), (1, 0)])  27.6 us
    ppermute x20, waiting for transfers between devices, onward(): return lax.ppermute(value, ('z', 'core'), pairs)  24 us
    all_to_all x1, blocking collectives, exchange(): return lax.all_to_all(value, plane, 0, 0, tiled=True)  15.3 us
    all_to_all x2, starting transfers between devices, exchange(): return lax.all_to_all(value, plane, 0, 0, tiled=True)  11.4 us
    pallas_call x2, Pallas kernels, first_product(): pl.pallas_call(functools.partial(first_kernel, choose), in_specs=[scalars...  7.32 us
    pallas_call x2, Pallas kernels, merged_product(): pl.pallas_call(kernel, in_specs=[scalars] + [whole] * (len(done) + 1 + le...  7.11 us
    unnamed x20, local copies, waits for them, and re-layouts  7.04 us
  transfers between devices with their start and end apart: 38, of which 18 were waited for; matrix products, arithmetic and copies ran while one was open for 0% of the time, Pallas kernels for 12%

profile of v1, /device:TPU:1, one launch (start us, length us, event | category | flops | bytes accessed | tf_op | source)
XLA Modules:
  0.0 158.3 jit_solution(14578240932195961313)
XLA Ops:
  0.0 2.2 %broadcast_in_dim.11.refs_0_ = bf16[16,8,8,768]{3,2,1,0:T(8,128)(2,1)} broadcast(bf16[8,8,768]{2,1,0:T(8,128)(2,1)} %bitcast.10), dimensions={1,2,3} | broadcast | bytes 1671168 | tf_op jit(solution)/shard_map/broadcast_in_dim | solution.py:427
  2.2 7.7 %all-to-all-start = ((bf16[16,8,8,768]{3,2,1,0:T(8,128)(2,1)}), bf16[16,8,8,768]{3,2,1,0:T(8,128)(2,1)S(1)}, u32[]{:S(2)}, u32[]{:S(2)}) async-start(bf16[16,8,8,768]{3,2,1,0:T(8,128)(2,1)} %broadcast_in_dim.11.refs_0_), calls=%async_computation | async-start | bytes 3145728 | tf_op jit(solution)/shard_map/all_to_all | solution.py:425
  10.0 2.3 %copy-done = bf16[768,3072]{1,0:T(8,128)(2,1)S(1)} copy-done((bf16[768,3072]{1,0:T(8,128)(2,1)S(1)}, bf16[768,3072]{1,0:T(8,128)(2,1)}, u32[]{:S(2)}) %copy-start) | copy-done | bytes 4718616
  15.4 6.5 %collective-permute-start.3 = (f32[2,2,3072]{2,1,0:T(2,128)S(1)}, f32[2,2,3072]{2,1,0:T(2,128)S(1)}, u32[]{:S(2)}, u32[]{:S(2)}) collective-permute-start(f32[2,2,3072]{2,1,0:T(2,128)S(1)} %pad_maximum_fusion.3.refs_0_), channel_id=1, source_target_pairs={{0,96},{16,176},{32,128},{48,208},{64,160},{80,240},{96,192},{112,... | collective-permute-start | bytes 147464 | tf_op jit(solution)/shard_map/ppermute | solution.py:32
  22.7 4.5 %collective-permute-start.4 = (f32[2,3072]{1,0:T(2,128)S(1)}, f32[2,3072]{1,0:T(2,128)S(1)}, u32[]{:S(2)}, u32[]{:S(2)}) collective-permute-start(f32[2,3072]{1,0:T(2,128)S(1)} %shard_map.73), channel_id=1, source_target_pairs={{0,128},{16,144},{32,160},{48,176},{64,192},{80,208},{96,224},{112... | collective-permute-start | bytes 73736 | tf_op jit(solution)/shard_map/ppermute | solution.py:32
  27.1 2.4 %collective-permute-done.4 = f32[2,3072]{1,0:T(2,128)S(1)} collective-permute-done((f32[2,3072]{1,0:T(2,128)S(1)}, f32[2,3072]{1,0:T(2,128)S(1)}, u32[]{:S(2)}, u32[]{:S(2)}) %collective-permute-start.4) | collective-permute-done | bytes 24608 | tf_op jit(solution)/shard_map/ppermute | solution.py:32
  29.7 3.3 %collective-permute-start.5 = (f32[7,2,3072]{2,1,0:T(2,128)S(1)}, f32[7,2,3072]{2,1,0:T(2,128)S(1)}, u32[]{:S(2)}, u32[]{:S(2)}) collective-permute-start(f32[7,2,3072]{2,1,0:T(2,128)S(1)} %pad_maximum_fusion.2.refs_1_), channel_id=1, source_target_pairs={{0,16},{16,0},{1,17},{17,1},{2,18},{18,2},{3,19},{19,3},{4,20},{20... | collective-permute-start | bytes 516104 | tf_op jit(solution)/shard_map/ppermute | solution.py:24
  34.0 2.3 %copy-done.1 = bf16[768,3072]{1,0:T(8,128)(2,1)S(1)} copy-done((bf16[768,3072]{1,0:T(8,128)(2,1)S(1)}, bf16[768,3072]{1,0:T(8,128)(2,1)}, u32[]{:S(2)}) %copy-start.1) | copy-done | bytes 4718616
  36.3 2.9 %shard_map.74 = (bf16[192,3200]{1,0:T(8,128)(2,1)S(1)}, bf16[192,3200]{1,0:T(8,128)(2,1)S(1)}) custom-call(s32[2]{0:T(128)S(1)} %pad_add_fusion.place.refs_0_, bf16[16,8,8,768]{3,2,1,0:T(8,128)(2,1)S(1)} %all-to-all-done.gathered, f32[1,768]{1,0:T(1,128)S(1)} %reshape.17.gain, bf16[768,3072]{1,0:T(8,128)(2,1)S(1)} %copy-done.1, ...), custom_call_target="tpu_custom_call" | custom-call | flops 1811939328 | bytes 7667712 | tf_op jit(solution)/shard_map/pallas_call | solution.py:150
  40.7 4.4 %shard_map.75 = (bf16[256,3200]{1,0:T(8,128)(2,1)S(1)}, bf16[384,3200]{1,0:T(8,128)(2,1)S(1)}) custom-call(s32[2]{0:T(128)S(1)} %pad_add_fusion.place.refs_0_, bf16[16,8,8,768]{3,2,1,0:T(8,128)(2,1)S(1)} %all-to-all-done.gathered, f32[1,768]{1,0:T(1,128)S(1)} %reshape.17.gain, bf16[768,3072]{1,0:T(8,128)(2,1)S(1)} %copy-done.1, ...), custom_call_target="tpu_custom_call" | custom-call | flops 3019898880 | bytes 9633792 | tf_op jit(solution)/shard_map/pallas_call | solution.py:150
  45.3 5.7 %collective-permute-start.8 = (bf16[32,3200]{1,0:T(8,128)(2,1)S(1)}, bf16[32,3200]{1,0:T(8,128)(2,1)S(1)}, u32[]{:S(2)}, u32[]{:S(2)}) collective-permute-start(bf16[32,3200]{1,0:T(8,128)(2,1)S(1)} %shard_map.76), channel_id=1, source_target_pairs={{0,32},{16,240},{32,64},{48,16},{64,96},{80,48},{96,128},{112,80},... | collective-permute-start | bytes 614408 | tf_op jit(solution)/shard_map/ppermute | solution.py:32
  53.8 3.2 %collective-permute-start.9 = (bf16[64,3200]{1,0:T(8,128)(2,1)S(1)}, bf16[64,3200]{1,0:T(8,128)(2,1)S(1)}, u32[]{:S(2)}, u32[]{:S(2)}) collective-permute-start(bf16[64,3200]{1,0:T(8,128)(2,1)S(1)} %shard_map.77), channel_id=1, source_target_pairs={{0,32},{16,240},{32,64},{48,16},{64,96},{80,48},{96,128},{112,80},... | collective-permute-start | bytes 1228808 | tf_op jit(solution)/shard_map/ppermute | solution.py:32
  57.2 2.0 %collective-permute-start.19 = (bf16[64,3200]{1,0:T(8,128)(2,1)S(1)}, bf16[64,3200]{1,0:T(8,128)(2,1)S(1)}, u32[]{:S(2)}, u32[]{:S(2)}) collective-permute-start(bf16[64,3200]{1,0:T(8,128)(2,1)S(1)} %shard_map.83), channel_id=1, source_target_pairs={{0,32},{16,240},{32,64},{48,16},{64,96},{80,48},{96,128},{112,80},... | collective-permute-start | bytes 1228808 | tf_op jit(solution)/shard_map/ppermute | solution.py:32
  59.2 2.7 %collective-permute-done.9.moving = bf16[64,3200]{1,0:T(8,128)(2,1)S(1)} collective-permute-done((bf16[64,3200]{1,0:T(8,128)(2,1)S(1)}, bf16[64,3200]{1,0:T(8,128)(2,1)S(1)}, u32[]{:S(2)}, u32[]{:S(2)}) %collective-permute-start.9) | collective-permute-done | bytes 409632 | tf_op jit(solution)/shard_map/ppermute | solution.py:32
  62.1 3.2 %collective-permute-start.10 = (bf16[64,3200]{1,0:T(8,128)(2,1)S(1)}, bf16[64,3200]{1,0:T(8,128)(2,1)S(1)}, u32[]{:S(2)}, u32[]{:S(2)}) collective-permute-start(bf16[64,3200]{1,0:T(8,128)(2,1)S(1)} %shard_map.78), channel_id=1, source_target_pairs={{0,32},{16,240},{32,64},{48,16},{64,96},{80,48},{96,128},{112,80},... | collective-permute-start | bytes 1228808 | tf_op jit(solution)/shard_map/ppermute | solution.py:32
  66.5 3.2 %collective-permute-start.20 = (bf16[64,3200]{1,0:T(8,128)(2,1)S(1)}, bf16[64,3200]{1,0:T(8,128)(2,1)S(1)}, u32[]{:S(2)}, u32[]{:S(2)}) collective-permute-start(bf16[64,3200]{1,0:T(8,128)(2,1)S(1)} %shard_map.84), channel_id=1, source_target_pairs={{0,32},{16,240},{32,64},{48,16},{64,96},{80,48},{96,128},{112,80},... | collective-permute-start | bytes 1228808 | tf_op jit(solution)/shard_map/ppermute | solution.py:32
  70.9 3.2 %collective-permute-start.11 = (bf16[64,3200]{1,0:T(8,128)(2,1)S(1)}, bf16[64,3200]{1,0:T(8,128)(2,1)S(1)}, u32[]{:S(2)}, u32[]{:S(2)}) collective-permute-start(bf16[64,3200]{1,0:T(8,128)(2,1)S(1)} %shard_map.79), channel_id=1, source_target_pairs={{0,32},{16,240},{32,64},{48,16},{64,96},{80,48},{96,128},{112,80},... | collective-permute-start | bytes 1228808 | tf_op jit(solution)/shard_map/ppermute | solution.py:32
  75.3 3.2 %collective-permute-start.21 = (bf16[64,3200]{1,0:T(8,128)(2,1)S(1)}, bf16[64,3200]{1,0:T(8,128)(2,1)S(1)}, u32[]{:S(2)}, u32[]{:S(2)}) collective-permute-start(bf16[64,3200]{1,0:T(8,128)(2,1)S(1)} %shard_map.85), channel_id=1, source_target_pairs={{0,32},{16,240},{32,64},{48,16},{64,96},{80,48},{96,128},{112,80},... | collective-permute-start | bytes 1228808 | tf_op jit(solution)/shard_map/ppermute | solution.py:32
  79.6 4.3 %collective-permute-start.12 = (bf16[32,3200]{1,0:T(8,128)(2,1)S(1)}, bf16[32,3200]{1,0:T(8,128)(2,1)S(1)}, u32[]{:S(2)}, u32[]{:S(2)}) collective-permute-start(bf16[32,3200]{1,0:T(8,128)(2,1)S(1)} %shard_map.80), channel_id=1, source_target_pairs={{0,16},{16,0},{1,17},{17,1},{2,18},{18,2},{3,19},{19,3},{4,20},{20... | collective-permute-start | bytes 614408 | tf_op jit(solution)/shard_map/ppermute | solution.py:24
  84.0 4.3 %collective-permute-start.22 = (bf16[32,3200]{1,0:T(8,128)(2,1)S(1)}, bf16[32,3200]{1,0:T(8,128)(2,1)S(1)}, u32[]{:S(2)}, u32[]{:S(2)}) collective-permute-start(bf16[32,3200]{1,0:T(8,128)(2,1)S(1)} %shard_map.86), channel_id=1, source_target_pairs={{0,16},{16,0},{1,17},{17,1},{2,18},{18,2},{3,19},{19,3},{4,20},{20... | collective-permute-start | bytes 614408 | tf_op jit(solution)/shard_map/ppermute | solution.py:24
  93.4 5.8 %collective-permute-done.14.refs_3_ = bf16[64,3072]{1,0:T(8,128)(2,1)S(1)} collective-permute-done((bf16[64,3072]{1,0:T(8,128)(2,1)S(1)}, bf16[64,3072]{1,0:T(8,128)(2,1)S(1)}, u32[]{:S(2)}, u32[]{:S(2)}) %collective-permute-start.14) | collective-permute-done | bytes 393248 | tf_op jit(solution)/shard_map/ppermute | solution.py:32
  100.2 3.3 %collective-permute-done.24.refs_8_ = bf16[64,3072]{1,0:T(8,128)(2,1)S(1)} collective-permute-done((bf16[64,3072]{1,0:T(8,128)(2,1)S(1)}, bf16[64,3072]{1,0:T(8,128)(2,1)S(1)}, u32[]{:S(2)}, u32[]{:S(2)}) %collective-permute-start.24) | collective-permute-done | bytes 393248 | tf_op jit(solution)/shard_map/ppermute | solution.py:32
  105.6 2.1 %collective-permute-done.15.refs_4_ = bf16[64,3072]{1,0:T(8,128)(2,1)S(1)} collective-permute-done((bf16[64,3072]{1,0:T(8,128)(2,1)S(1)}, bf16[64,3072]{1,0:T(8,128)(2,1)S(1)}, u32[]{:S(2)}, u32[]{:S(2)}) %collective-permute-start.15) | collective-permute-done | bytes 393248 | tf_op jit(solution)/shard_map/ppermute | solution.py:32
  107.7 2.7 %collective-permute-start.17 = (bf16[64,3072]{1,0:T(8,128)(2,1)S(1)}, bf16[64,3072]{1,0:T(8,128)(2,1)S(1)}, u32[]{:S(2)}, u32[]{:S(2)}) collective-permute-start(bf16[64,3072]{1,0:T(8,128)(2,1)S(1)} %collective-permute-done.15.refs_4_), channel_id=1, source_target_pairs={{0,16},{16,0},{1,17},{17,1},{2,18},{18,2},{3,19},{19,3},{4,20},{20... | collective-permute-start | bytes 1179656 | tf_op jit(solution)/shard_map/ppermute | solution.py:24
  111.9 2.7 %collective-permute-start.27 = (bf16[64,3072]{1,0:T(8,128)(2,1)S(1)}, bf16[64,3072]{1,0:T(8,128)(2,1)S(1)}, u32[]{:S(2)}, u32[]{:S(2)}) collective-permute-start(bf16[64,3072]{1,0:T(8,128)(2,1)S(1)} %collective-permute-done.25.refs_9_), channel_id=1, source_target_pairs={{0,16},{16,0},{1,17},{17,1},{2,18},{18,2},{3,19},{19,3},{4,20},{20... | collective-permute-start | bytes 1179656 | tf_op jit(solution)/shard_map/ppermute | solution.py:24
  115.9 5.3 %shard_map.89.refs_0_ = bf16[16,5,8,768]{3,2,1,0:T(8,128)(2,1)} custom-call(s32[2]{0:T(128)S(1)} %pad_add_fusion.place.refs_0_, bf16[3072,768]{1,0:T(8,128)(2,1)S(1)} %bitcast.9, bf16[64,3072]{1,0:T(8,128)(2,1)S(1)} %pad_maximum_fusion.refs_2_, bf16[64,3072]{1,0:T(8,128)(2,1)S(1)} %collective-permute-done.14.refs_3_, ...), custom_call_target="tpu_custom_call" | custom-call | flops 3019898880 | bytes 9633792 | tf_op jit(solution)/shard_map/pallas_call | solution.py:367
  121.3 3.6 %all-to-all-start.1 = ((bf16[16,5,8,768]{3,2,1,0:T(8,128)(2,1)}), bf16[16,5,8,768]{3,2,1,0:T(8,128)(2,1)S(1)}, u32[]{:S(2)}, u32[]{:S(2)}) async-start(bf16[16,5,8,768]{3,2,1,0:T(8,128)(2,1)} %shard_map.89.refs_0_), calls=%async_computation.1 | async-start | bytes 1966080 | tf_op jit(solution)/shard_map/all_to_all | solution.py:425
  125.8 2.1 %collective-permute-start.31 = (bf16[64,3072]{1,0:T(8,128)(2,1)S(1)}, bf16[64,3072]{1,0:T(8,128)(2,1)S(1)}, u32[]{:S(2)}, u32[]{:S(2)}) collective-permute-start(bf16[64,3072]{1,0:T(8,128)(2,1)S(1)} %collective-permute-done.30.refs_2_.value), channel_id=1, source_target_pairs={{0,16},{16,0},{1,17},{17,1},{2,18},{18,2},{3,19},{19,3},{4,20},{20... | collective-permute-start | bytes 1179656 | tf_op jit(solution)/shard_map/ppermute | solution.py:24
  129.7 2.3 %copy-done.2 = bf16[3072,768]{1,0:T(8,128)(2,1)S(1)} copy-done((bf16[3072,768]{1,0:T(8,128)(2,1)S(1)}, bf16[3072,768]{1,0:T(8,128)(2,1)}, u32[]{:S(2)}) %copy-start.2) | copy-done | bytes 4718616
  135.0 2.1 %collective-permute-start.35 = (bf16[32,3072]{1,0:T(8,128)(2,1)S(1)}, bf16[32,3072]{1,0:T(8,128)(2,1)S(1)}, u32[]{:S(2)}, u32[]{:S(2)}) collective-permute-start(bf16[32,3072]{1,0:T(8,128)(2,1)S(1)} %shard_map.94.refs_5_), channel_id=1, source_target_pairs={{0,16},{16,0},{1,17},{17,1},{2,18},{18,2},{3,19},{19,3},{4,20},{20... | collective-permute-start | bytes 589832 | tf_op jit(solution)/shard_map/ppermute | solution.py:24
  140.9 15.3 %all_to_all.15.far = bf16[16,3,8,768]{3,2,1,0:T(8,128)(2,1)S(1)} all-to-all(bf16[16,3,8,768]{3,2,1,0:T(8,128)(2,1)S(1)} %shard_map.95), channel_id=1, replica_groups=mesh['z'=8,'core'=2,'y'=4,'x'=4] {'y','x'}, dimensions={0} | all-to-all | bytes 1179648 | tf_op jit(solution)/shard_map/all_to_all | solution.py:425
  156.3 2.0 %shard_map.96 = bf16[8,8,768]{2,1,0:T(8,128)(2,1)} custom-call(s32[2]{0:T(128)S(1)} %pad_add_fusion.place.refs_0_, bf16[16,5,8,768]{3,2,1,0:T(8,128)(2,1)S(1)} %all-to-all-done.1.near, bf16[16,3,8,768]{3,2,1,0:T(8,128)(2,1)S(1)} %all_to_all.15.far, f32[8,8,768]{2,1,0:T(8,128)S(1)} %shard_map.88.refs_12_.base), custom_call_target="tpu_custom_call" | custom-call | tf_op jit(solution)/shard_map/pallas_call | solution.py:407
  (99 shorter events, 34.9 us)
Async XLA Ops:
  2.2 31.8 %all-to-all-start = ((bf16[16,8,8,768]{3,2,1,0:T(8,128)(2,1)}), bf16[16,8,8,768]{3,2,1,0:T(8,128)(2,1)S(1)}, u32[]{:S(2)}, u32[]{:S(2)}) async-start(bf16[16,8,8,768]{3,2,1,0:T(8,128)(2,1)} %broadcast_in_dim.11.refs_0_), calls=%async_computation | async-start | bytes 3145728 | tf_op jit(solution)/shard_map/all_to_all | solution.py:425
  15.4 14.2 %collective-permute-start.3 = (f32[2,2,3072]{2,1,0:T(2,128)S(1)}, f32[2,2,3072]{2,1,0:T(2,128)S(1)}, u32[]{:S(2)}, u32[]{:S(2)}) collective-permute-start(f32[2,2,3072]{2,1,0:T(2,128)S(1)} %pad_maximum_fusion.3.refs_0_), channel_id=1, source_target_pairs={{0,96},{16,176},{32,128},{48,208},{64,160},{80,240},{96,192},{112,... | collective-permute-start | bytes 147464 | tf_op jit(solution)/shard_map/ppermute | solution.py:32
  21.9 7.6 %collective-permute-start.2 = (f32[2,2,3072]{2,1,0:T(2,128)S(1)}, f32[2,2,3072]{2,1,0:T(2,128)S(1)}, u32[]{:S(2)}, u32[]{:S(2)}) collective-permute-start(f32[2,2,3072]{2,1,0:T(2,128)S(1)} %pad_maximum_fusion.3.refs_0_), channel_id=1, source_target_pairs={{0,64},{16,208},{32,96},{48,240},{64,128},{80,16},{96,160},{112,48... | collective-permute-start | bytes 147464 | tf_op jit(solution)/shard_map/ppermute | solution.py:32
  22.2 7.4 %collective-permute-start.1 = (f32[2,2,3072]{2,1,0:T(2,128)S(1)}, f32[2,2,3072]{2,1,0:T(2,128)S(1)}, u32[]{:S(2)}, u32[]{:S(2)}) collective-permute-start(f32[2,2,3072]{2,1,0:T(2,128)S(1)} %pad_maximum_fusion.3.refs_0_), channel_id=1, source_target_pairs={{0,32},{16,240},{32,64},{48,16},{64,96},{80,48},{96,128},{112,80},... | collective-permute-start | bytes 147464 | tf_op jit(solution)/shard_map/ppermute | solution.py:32
  22.7 6.9 %collective-permute-start.4 = (f32[2,3072]{1,0:T(2,128)S(1)}, f32[2,3072]{1,0:T(2,128)S(1)}, u32[]{:S(2)}, u32[]{:S(2)}) collective-permute-start(f32[2,3072]{1,0:T(2,128)S(1)} %shard_map.73), channel_id=1, source_target_pairs={{0,128},{16,144},{32,160},{48,176},{64,192},{80,208},{96,224},{112... | collective-permute-start | bytes 73736 | tf_op jit(solution)/shard_map/ppermute | solution.py:32
  29.7 4.3 %collective-permute-start.5 = (f32[7,2,3072]{2,1,0:T(2,128)S(1)}, f32[7,2,3072]{2,1,0:T(2,128)S(1)}, u32[]{:S(2)}, u32[]{:S(2)}) collective-permute-start(f32[7,2,3072]{2,1,0:T(2,128)S(1)} %pad_maximum_fusion.2.refs_1_), channel_id=1, source_target_pairs={{0,16},{16,0},{1,17},{17,1},{2,18},{18,2},{3,19},{19,3},{4,20},{20... | collective-permute-start | bytes 516104 | tf_op jit(solution)/shard_map/ppermute | solution.py:24
  39.2 6.0 %collective-permute-start.7 = (bf16[192,3200]{1,0:T(8,128)(2,1)S(1)}, bf16[192,3200]{1,0:T(8,128)(2,1)S(1)}, u32[]{:S(2)}, u32[]{:S(2)}) collective-permute-start(bf16[192,3200]{1,0:T(8,128)(2,1)S(1)} %get-tuple-element.11.refs_0_), channel_id=1, source_target_pairs={{0,16},{16,0},{1,17},{17,1},{2,18},{18,2},{3,19},{19,3},{4,20},{20... | collective-permute-start | bytes 3686408 | tf_op jit(solution)/shard_map/ppermute | solution.py:24
  45.1 14.1 %collective-permute-start.6 = (bf16[256,3200]{1,0:T(8,128)(2,1)S(1)}, bf16[256,3200]{1,0:T(8,128)(2,1)S(1)}, u32[]{:S(2)}, u32[]{:S(2)}) collective-permute-start(bf16[256,3200]{1,0:T(8,128)(2,1)S(1)} %get-tuple-element.13), channel_id=1, source_target_pairs={{0,16},{16,0},{1,17},{17,1},{2,18},{18,2},{3,19},{19,3},{4,20},{20... | collective-permute-start | bytes 4915208 | tf_op jit(solution)/shard_map/ppermute | solution.py:24
  45.3 8.4 %collective-permute-start.8 = (bf16[32,3200]{1,0:T(8,128)(2,1)S(1)}, bf16[32,3200]{1,0:T(8,128)(2,1)S(1)}, u32[]{:S(2)}, u32[]{:S(2)}) collective-permute-start(bf16[32,3200]{1,0:T(8,128)(2,1)S(1)} %shard_map.76), channel_id=1, source_target_pairs={{0,32},{16,240},{32,64},{48,16},{64,96},{80,48},{96,128},{112,80},... | collective-permute-start | bytes 614408 | tf_op jit(solution)/shard_map/ppermute | solution.py:32
  51.1 6.0 %collective-permute-start.18 = (bf16[32,3200]{1,0:T(8,128)(2,1)S(1)}, bf16[32,3200]{1,0:T(8,128)(2,1)S(1)}, u32[]{:S(2)}, u32[]{:S(2)}) collective-permute-start(bf16[32,3200]{1,0:T(8,128)(2,1)S(1)} %shard_map.82), channel_id=1, source_target_pairs={{0,32},{16,240},{32,64},{48,16},{64,96},{80,48},{96,128},{112,80},... | collective-permute-start | bytes 614408 | tf_op jit(solution)/shard_map/ppermute | solution.py:32
  53.8 8.1 %collective-permute-start.9 = (bf16[64,3200]{1,0:T(8,128)(2,1)S(1)}, bf16[64,3200]{1,0:T(8,128)(2,1)S(1)}, u32[]{:S(2)}, u32[]{:S(2)}) collective-permute-start(bf16[64,3200]{1,0:T(8,128)(2,1)S(1)} %shard_map.77), channel_id=1, source_target_pairs={{0,32},{16,240},{32,64},{48,16},{64,96},{80,48},{96,128},{112,80},... | collective-permute-start | bytes 1228808 | tf_op jit(solution)/shard_map/ppermute | solution.py:32
  57.2 9.1 %collective-permute-start.19 = (bf16[64,3200]{1,0:T(8,128)(2,1)S(1)}, bf16[64,3200]{1,0:T(8,128)(2,1)S(1)}, u32[]{:S(2)}, u32[]{:S(2)}) collective-permute-start(bf16[64,3200]{1,0:T(8,128)(2,1)S(1)} %shard_map.83), channel_id=1, source_target_pairs={{0,32},{16,240},{32,64},{48,16},{64,96},{80,48},{96,128},{112,80},... | collective-permute-start | bytes 1228808 | tf_op jit(solution)/shard_map/ppermute | solution.py:32
  62.1 8.6 %collective-permute-start.10 = (bf16[64,3200]{1,0:T(8,128)(2,1)S(1)}, bf16[64,3200]{1,0:T(8,128)(2,1)S(1)}, u32[]{:S(2)}, u32[]{:S(2)}) collective-permute-start(bf16[64,3200]{1,0:T(8,128)(2,1)S(1)} %shard_map.78), channel_id=1, source_target_pairs={{0,32},{16,240},{32,64},{48,16},{64,96},{80,48},{96,128},{112,80},... | collective-permute-start | bytes 1228808 | tf_op jit(solution)/shard_map/ppermute | solution.py:32
  66.5 8.6 %collective-permute-start.20 = (bf16[64,3200]{1,0:T(8,128)(2,1)S(1)}, bf16[64,3200]{1,0:T(8,128)(2,1)S(1)}, u32[]{:S(2)}, u32[]{:S(2)}) collective-permute-start(bf16[64,3200]{1,0:T(8,128)(2,1)S(1)} %shard_map.84), channel_id=1, source_target_pairs={{0,32},{16,240},{32,64},{48,16},{64,96},{80,48},{96,128},{112,80},... | collective-permute-start | bytes 1228808 | tf_op jit(solution)/shard_map/ppermute | solution.py:32
  70.9 8.6 %collective-permute-start.11 = (bf16[64,3200]{1,0:T(8,128)(2,1)S(1)}, bf16[64,3200]{1,0:T(8,128)(2,1)S(1)}, u32[]{:S(2)}, u32[]{:S(2)}) collective-permute-start(bf16[64,3200]{1,0:T(8,128)(2,1)S(1)} %shard_map.79), channel_id=1, source_target_pairs={{0,32},{16,240},{32,64},{48,16},{64,96},{80,48},{96,128},{112,80},... | collective-permute-start | bytes 1228808 | tf_op jit(solution)/shard_map/ppermute | solution.py:32
  75.3 8.6 %collective-permute-start.21 = (bf16[64,3200]{1,0:T(8,128)(2,1)S(1)}, bf16[64,3200]{1,0:T(8,128)(2,1)S(1)}, u32[]{:S(2)}, u32[]{:S(2)}) collective-permute-start(bf16[64,3200]{1,0:T(8,128)(2,1)S(1)} %shard_map.85), channel_id=1, source_target_pairs={{0,32},{16,240},{32,64},{48,16},{64,96},{80,48},{96,128},{112,80},... | collective-permute-start | bytes 1228808 | tf_op jit(solution)/shard_map/ppermute | solution.py:32
  79.6 8.7 %collective-permute-start.12 = (bf16[32,3200]{1,0:T(8,128)(2,1)S(1)}, bf16[32,3200]{1,0:T(8,128)(2,1)S(1)}, u32[]{:S(2)}, u32[]{:S(2)}) collective-permute-start(bf16[32,3200]{1,0:T(8,128)(2,1)S(1)} %shard_map.80), channel_id=1, source_target_pairs={{0,16},{16,0},{1,17},{17,1},{2,18},{18,2},{3,19},{19,3},{4,20},{20... | collective-permute-start | bytes 614408 | tf_op jit(solution)/shard_map/ppermute | solution.py:24
  84.0 6.1 %collective-permute-start.22 = (bf16[32,3200]{1,0:T(8,128)(2,1)S(1)}, bf16[32,3200]{1,0:T(8,128)(2,1)S(1)}, u32[]{:S(2)}, u32[]{:S(2)}) collective-permute-start(bf16[32,3200]{1,0:T(8,128)(2,1)S(1)} %shard_map.86), channel_id=1, source_target_pairs={{0,16},{16,0},{1,17},{17,1},{2,18},{18,2},{3,19},{19,3},{4,20},{20... | collective-permute-start | bytes 614408 | tf_op jit(solution)/shard_map/ppermute | solution.py:24
  92.2 7.0 %collective-permute-start.14 = (bf16[64,3072]{1,0:T(8,128)(2,1)S(1)}, bf16[64,3072]{1,0:T(8,128)(2,1)S(1)}, u32[]{:S(2)}, u32[]{:S(2)}) collective-permute-start(bf16[64,3072]{1,0:T(8,128)(2,1)S(1)} %pad_maximum_fusion.refs_2_), channel_id=1, source_target_pairs={{0,32},{16,240},{32,64},{48,16},{64,96},{80,48},{96,128},{112,80},... | collective-permute-start | bytes 1179656 | tf_op jit(solution)/shard_map/ppermute | solution.py:32
  93.3 10.1 %collective-permute-start.24 = (bf16[64,3072]{1,0:T(8,128)(2,1)S(1)}, bf16[64,3072]{1,0:T(8,128)(2,1)S(1)}, u32[]{:S(2)}, u32[]{:S(2)}) collective-permute-start(bf16[64,3072]{1,0:T(8,128)(2,1)S(1)} %pad_maximum_fusion.1.refs_7_), channel_id=1, source_target_pairs={{0,32},{16,240},{32,64},{48,16},{64,96},{80,48},{96,128},{112,80},... | collective-permute-start | bytes 1179656 | tf_op jit(solution)/shard_map/ppermute | solution.py:32
  99.2 8.4 %collective-permute-start.15 = (bf16[64,3072]{1,0:T(8,128)(2,1)S(1)}, bf16[64,3072]{1,0:T(8,128)(2,1)S(1)}, u32[]{:S(2)}, u32[]{:S(2)}) collective-permute-start(bf16[64,3072]{1,0:T(8,128)(2,1)S(1)} %collective-permute-done.14.refs_3_), channel_id=1, source_target_pairs={{0,32},{16,240},{32,64},{48,16},{64,96},{80,48},{96,128},{112,80},... | collective-permute-start | bytes 1179656 | tf_op jit(solution)/shard_map/ppermute | solution.py:32
  103.5 8.4 %collective-permute-start.25 = (bf16[64,3072]{1,0:T(8,128)(2,1)S(1)}, bf16[64,3072]{1,0:T(8,128)(2,1)S(1)}, u32[]{:S(2)}, u32[]{:S(2)}) collective-permute-start(bf16[64,3072]{1,0:T(8,128)(2,1)S(1)} %collective-permute-done.24.refs_8_), channel_id=1, source_target_pairs={{0,32},{16,240},{32,64},{48,16},{64,96},{80,48},{96,128},{112,80},... | collective-permute-start | bytes 1179656 | tf_op jit(solution)/shard_map/ppermute | solution.py:32
  104.4 10.3 %collective-permute-start.16 = (bf16[64,3072]{1,0:T(8,128)(2,1)S(1)}, bf16[64,3072]{1,0:T(8,128)(2,1)S(1)}, u32[]{:S(2)}, u32[]{:S(2)}) collective-permute-start(bf16[64,3072]{1,0:T(8,128)(2,1)S(1)} %collective-permute-done.14.refs_3_), channel_id=1, source_target_pairs={{0,16},{16,0},{1,17},{17,1},{2,18},{18,2},{3,19},{19,3},{4,20},{20... | collective-permute-start | bytes 1179656 | tf_op jit(solution)/shard_map/ppermute | solution.py:24
  105.6 9.2 %collective-permute-start.26 = (bf16[64,3072]{1,0:T(8,128)(2,1)S(1)}, bf16[64,3072]{1,0:T(8,128)(2,1)S(1)}, u32[]{:S(2)}, u32[]{:S(2)}) collective-permute-start(bf16[64,3072]{1,0:T(8,128)(2,1)S(1)} %collective-permute-done.24.refs_8_), channel_id=1, source_target_pairs={{0,16},{16,0},{1,17},{17,1},{2,18},{18,2},{3,19},{19,3},{4,20},{20... | collective-permute-start | bytes 1179656 | tf_op jit(solution)/shard_map/ppermute | solution.py:24
  107.7 7.1 %collective-permute-start.17 = (bf16[64,3072]{1,0:T(8,128)(2,1)S(1)}, bf16[64,3072]{1,0:T(8,128)(2,1)S(1)}, u32[]{:S(2)}, u32[]{:S(2)}) collective-permute-start(bf16[64,3072]{1,0:T(8,128)(2,1)S(1)} %collective-permute-done.15.refs_4_), channel_id=1, source_target_pairs={{0,16},{16,0},{1,17},{17,1},{2,18},{18,2},{3,19},{19,3},{4,20},{20... | collective-permute-start | bytes 1179656 | tf_op jit(solution)/shard_map/ppermute | solution.py:24
  111.9 4.0 %collective-permute-start.27 = (bf16[64,3072]{1,0:T(8,128)(2,1)S(1)}, bf16[64,3072]{1,0:T(8,128)(2,1)S(1)}, u32[]{:S(2)}, u32[]{:S(2)}) collective-permute-start(bf16[64,3072]{1,0:T(8,128)(2,1)S(1)} %collective-permute-done.25.refs_9_), channel_id=1, source_target_pairs={{0,16},{16,0},{1,17},{17,1},{2,18},{18,2},{3,19},{19,3},{4,20},{20... | collective-permute-start | bytes 1179656 | tf_op jit(solution)/shard_map/ppermute | solution.py:24
  114.6 10.3 %collective-permute-start.28 = (bf16[64,3072]{1,0:T(8,128)(2,1)S(1)}, bf16[64,3072]{1,0:T(8,128)(2,1)S(1)}, u32[]{:S(2)}, u32[]{:S(2)}) collective-permute-start(bf16[64,3072]{1,0:T(8,128)(2,1)S(1)} %collective-permute-done.15.refs_4_), channel_id=1, source_target_pairs={{0,32},{16,240},{32,64},{48,16},{64,96},{80,48},{96,128},{112,80},... | collective-permute-start | bytes 1179656 | tf_op jit(solution)/shard_map/ppermute | solution.py:32
  114.7 11.1 %collective-permute-start.30 = (bf16[64,3072]{1,0:T(8,128)(2,1)S(1)}, bf16[64,3072]{1,0:T(8,128)(2,1)S(1)}, u32[]{:S(2)}, u32[]{:S(2)}) collective-permute-start(bf16[64,3072]{1,0:T(8,128)(2,1)S(1)} %collective-permute-done.25.refs_9_), channel_id=1, source_target_pairs={{0,32},{16,240},{32,64},{48,16},{64,96},{80,48},{96,128},{112,80},... | collective-permute-start | bytes 1179656 | tf_op jit(solution)/shard_map/ppermute | solution.py:32
  121.3 19.7 %all-to-all-start.1 = ((bf16[16,5,8,768]{3,2,1,0:T(8,128)(2,1)}), bf16[16,5,8,768]{3,2,1,0:T(8,128)(2,1)S(1)}, u32[]{:S(2)}, u32[]{:S(2)}) async-start(bf16[16,5,8,768]{3,2,1,0:T(8,128)(2,1)} %shard_map.89.refs_0_), calls=%async_computation.1 | async-start | bytes 1966080 | tf_op jit(solution)/shard_map/all_to_all | solution.py:425
  124.9 4.7 %collective-permute-start.29 = (bf16[64,3072]{1,0:T(8,128)(2,1)S(1)}, bf16[64,3072]{1,0:T(8,128)(2,1)S(1)}, u32[]{:S(2)}, u32[]{:S(2)}) collective-permute-start(bf16[64,3072]{1,0:T(8,128)(2,1)S(1)} %collective-permute-done.28.refs_0_.value), channel_id=1, source_target_pairs={{0,16},{16,0},{1,17},{17,1},{2,18},{18,2},{3,19},{19,3},{4,20},{20... | collective-permute-start | bytes 1179656 | tf_op jit(solution)/shard_map/ppermute | solution.py:24
  127.9 5.7 %collective-permute-start.32 = (bf16[32,3072]{1,0:T(8,128)(2,1)S(1)}, bf16[32,3072]{1,0:T(8,128)(2,1)S(1)}, u32[]{:S(2)}, u32[]{:S(2)}) collective-permute-start(bf16[32,3072]{1,0:T(8,128)(2,1)S(1)} %shard_map.91), channel_id=1, source_target_pairs={{0,32},{16,240},{32,64},{48,16},{64,96},{80,48},{96,128},{112,80},... | collective-permute-start | bytes 589832 | tf_op jit(solution)/shard_map/ppermute | solution.py:32
  128.0 7.0 %collective-permute-start.34 = (bf16[32,3072]{1,0:T(8,128)(2,1)S(1)}, bf16[32,3072]{1,0:T(8,128)(2,1)S(1)}, u32[]{:S(2)}, u32[]{:S(2)}) collective-permute-start(bf16[32,3072]{1,0:T(8,128)(2,1)S(1)} %shard_map.93), channel_id=1, source_target_pairs={{0,32},{16,240},{32,64},{48,16},{64,96},{80,48},{96,128},{112,80},... | collective-permute-start | bytes 589832 | tf_op jit(solution)/shard_map/ppermute | solution.py:32
  (16 other events, 154.7 us)

commit v2 on v1

--- a/solution.py
+++ b/solution.py
@@ -281,9 +281,13 @@
 def product_kernel(*refs):
     tiles, weight, out, held = refs[:-3], refs[-3], refs[-2], refs[-1]
     left = jnp.concatenate([tile[...] for tile in tiles])
-    total = jnp.dot(left, weight[...], preferred_element_type=jnp.float32)
-    out[...] = total.astype(jnp.bfloat16)
-    held[...] = weight[...]
+
+    def work(span):
+        total = jnp.dot(left, weight[:, span], preferred_element_type=jnp.float32)
+        out[:, span] = total.astype(jnp.bfloat16)
+        held[:, span] = weight[:, span]
+
+    columns(weight.shape[1], 256, work)
 
 
 def merge_kernel(slots, earlier, place, *refs):
@@ -307,7 +311,7 @@
                     out[base + i, number, :, span] = total[first : first + group].astype(jnp.bfloat16)
             old, new = old + early, new + 1 - early
 
-    columns(weight.shape[1], 256, work)
+    columns(weight.shape[1], 256 if earlier else weight.shape[1], work)
 
 
 def near_slots(core):
@@ -392,15 +396,15 @@
 
 def last_kernel(place, near, far, base, out):
     offsets = (0, -1, 1, -2, 2, -3, 3, 4)
-    for slot, steps in enumerate(offsets):
-        where = around(place[0], steps)
-        shares, number = (near, slot) if slot < 5 else (far, slot - 5)
-
-        def more(i, total):
-            return total + shares[i, number].astype(jnp.float32)
-
-        total = lax.fori_loop(0, shares.shape[0], more, base[where])
-        out[where] = total.astype(jnp.bfloat16)
+    where = [around(place[0], steps) for steps in offsets]
+
+    def more(i, totals):
+        shares = [near[i, slot] for slot in range(5)] + [far[i, slot] for slot in range(3)]
+        return tuple(total + share.astype(jnp.float32) for total, share in zip(totals, shares))
+
+    totals = lax.fori_loop(0, near.shape[0], more, tuple(base[number] for number in where))
+    for number, total in zip(where, totals):
+        out[number] = total.astype(jnp.bfloat16)
 
 
 def last_sum(place, near, far, base):

time: 159 us -> 158 us (level)
  transfers between devices with their start and end apart: 38 -> 38, of which waited for: 18 -> 19; matrix products, arithmetic and copies ran while one was open for 0% -> 0% of each run, Pallas kernels for 12% -> 12%
where the time goes in v2:
time: 158 us
  starting transfers between devices  78.7 us (50%)
  waiting for transfers between devices  30.2 us (19%)
  Pallas kernels  23.2 us (15%)
  blocking collectives  15.9 us (10%)
  local copies, waits for them, and re-layouts  9.26 us (6%)
    ppermute x20, starting transfers between devices, onward(): return lax.ppermute(value, ('z', 'core'), pairs)  39.7 us
    ppermute x16, starting transfers between devices, swap(): return lax.ppermute(value, 'core', [(0, 1), (1, 0)])  27.7 us
    ppermute x20, waiting for transfers between devices, onward(): return lax.ppermute(value, ('z', 'core'), pairs)  24.6 us
    all_to_all x1, blocking collectives, exchange(): return lax.all_to_all(value, plane, 0, 0, tiled=True)  15.9 us
    all_to_all x2, starting transfers between devices, exchange(): return lax.all_to_all(value, plane, 0, 0, tiled=True)  11.4 us
    pallas_call x2, Pallas kernels, first_product(): pl.pallas_call(functools.partial(first_kernel, choose), in_specs=[scalars...  7.32 us
    unnamed x20, local copies, waits for them, and re-layouts  7.04 us
    pallas_call x2, Pallas kernels, merged_product(): pl.pallas_call(kernel, in_specs=[scalars] + [whole] * (len(done) + 1 + le...  6.52 us
  transfers between devices with their start and end apart: 38, of which 19 were waited for; matrix products, arithmetic and copies ran while one was open for 0% of the time, Pallas kernels for 12%

profile of v2, /device:TPU:1, one launch (start us, length us, event | category | flops | bytes accessed | tf_op | source)
XLA Modules:
  0.0 157.8 jit_solution(6400194718017149582)
XLA Ops:
  0.0 2.2 %broadcast_in_dim.11.refs_0_ = bf16[16,8,8,768]{3,2,1,0:T(8,128)(2,1)} broadcast(bf16[8,8,768]{2,1,0:T(8,128)(2,1)} %bitcast.10), dimensions={1,2,3} | broadcast | bytes 1671168 | tf_op jit(solution)/shard_map/broadcast_in_dim | solution.py:431
  2.2 7.7 %all-to-all-start = ((bf16[16,8,8,768]{3,2,1,0:T(8,128)(2,1)}), bf16[16,8,8,768]{3,2,1,0:T(8,128)(2,1)S(1)}, u32[]{:S(2)}, u32[]{:S(2)}) async-start(bf16[16,8,8,768]{3,2,1,0:T(8,128)(2,1)} %broadcast_in_dim.11.refs_0_), calls=%async_computation | async-start | bytes 3145728 | tf_op jit(solution)/shard_map/all_to_all | solution.py:429
  10.0 2.3 %copy-done = bf16[768,3072]{1,0:T(8,128)(2,1)S(1)} copy-done((bf16[768,3072]{1,0:T(8,128)(2,1)S(1)}, bf16[768,3072]{1,0:T(8,128)(2,1)}, u32[]{:S(2)}) %copy-start) | copy-done | bytes 4718616
  15.4 6.5 %collective-permute-start.3 = (f32[2,2,3072]{2,1,0:T(2,128)S(1)}, f32[2,2,3072]{2,1,0:T(2,128)S(1)}, u32[]{:S(2)}, u32[]{:S(2)}) collective-permute-start(f32[2,2,3072]{2,1,0:T(2,128)S(1)} %pad_maximum_fusion.3.refs_0_), channel_id=1, source_target_pairs={{0,96},{16,176},{32,128},{48,208},{64,160},{80,240},{96,192},{112,... | collective-permute-start | bytes 147464 | tf_op jit(solution)/shard_map/ppermute | solution.py:32
  22.7 4.5 %collective-permute-start.4 = (f32[2,3072]{1,0:T(2,128)S(1)}, f32[2,3072]{1,0:T(2,128)S(1)}, u32[]{:S(2)}, u32[]{:S(2)}) collective-permute-start(f32[2,3072]{1,0:T(2,128)S(1)} %shard_map.73), channel_id=1, source_target_pairs={{0,128},{16,144},{32,160},{48,176},{64,192},{80,208},{96,224},{112... | collective-permute-start | bytes 73736 | tf_op jit(solution)/shard_map/ppermute | solution.py:32
  27.1 2.4 %collective-permute-done.4 = f32[2,3072]{1,0:T(2,128)S(1)} collective-permute-done((f32[2,3072]{1,0:T(2,128)S(1)}, f32[2,3072]{1,0:T(2,128)S(1)}, u32[]{:S(2)}, u32[]{:S(2)}) %collective-permute-start.4) | collective-permute-done | bytes 24608 | tf_op jit(solution)/shard_map/ppermute | solution.py:32
  29.7 3.3 %collective-permute-start.5 = (f32[7,2,3072]{2,1,0:T(2,128)S(1)}, f32[7,2,3072]{2,1,0:T(2,128)S(1)}, u32[]{:S(2)}, u32[]{:S(2)}) collective-permute-start(f32[7,2,3072]{2,1,0:T(2,128)S(1)} %pad_maximum_fusion.2.refs_1_), channel_id=1, source_target_pairs={{0,16},{16,0},{1,17},{17,1},{2,18},{18,2},{3,19},{19,3},{4,20},{20... | collective-permute-start | bytes 516104 | tf_op jit(solution)/shard_map/ppermute | solution.py:24
  34.0 2.3 %copy-done.1 = bf16[768,3072]{1,0:T(8,128)(2,1)S(1)} copy-done((bf16[768,3072]{1,0:T(8,128)(2,1)S(1)}, bf16[768,3072]{1,0:T(8,128)(2,1)}, u32[]{:S(2)}) %copy-start.1) | copy-done | bytes 4718616
  36.3 2.9 %shard_map.74 = (bf16[192,3200]{1,0:T(8,128)(2,1)S(1)}, bf16[192,3200]{1,0:T(8,128)(2,1)S(1)}) custom-call(s32[2]{0:T(128)S(1)} %pad_add_fusion.place.refs_0_, bf16[16,8,8,768]{3,2,1,0:T(8,128)(2,1)S(1)} %all-to-all-done.gathered, f32[1,768]{1,0:T(1,128)S(1)} %reshape.17.gain, bf16[768,3072]{1,0:T(8,128)(2,1)S(1)} %copy-done.1, ...), custom_call_target="tpu_custom_call" | custom-call | flops 1811939328 | bytes 7667712 | tf_op jit(solution)/shard_map/pallas_call | solution.py:150
  40.7 4.4 %shard_map.75 = (bf16[256,3200]{1,0:T(8,128)(2,1)S(1)}, bf16[384,3200]{1,0:T(8,128)(2,1)S(1)}) custom-call(s32[2]{0:T(128)S(1)} %pad_add_fusion.place.refs_0_, bf16[16,8,8,768]{3,2,1,0:T(8,128)(2,1)S(1)} %all-to-all-done.gathered, f32[1,768]{1,0:T(1,128)S(1)} %reshape.17.gain, bf16[768,3072]{1,0:T(8,128)(2,1)S(1)} %copy-done.1, ...), custom_call_target="tpu_custom_call" | custom-call | flops 3019898880 | bytes 9633792 | tf_op jit(solution)/shard_map/pallas_call | solution.py:150
  45.3 5.7 %collective-permute-start.8 = (bf16[32,3200]{1,0:T(8,128)(2,1)S(1)}, bf16[32,3200]{1,0:T(8,128)(2,1)S(1)}, u32[]{:S(2)}, u32[]{:S(2)}) collective-permute-start(bf16[32,3200]{1,0:T(8,128)(2,1)S(1)} %shard_map.76), channel_id=1, source_target_pairs={{0,32},{16,240},{32,64},{48,16},{64,96},{80,48},{96,128},{112,80},... | collective-permute-start | bytes 614408 | tf_op jit(solution)/shard_map/ppermute | solution.py:32
  53.8 3.2 %collective-permute-start.9 = (bf16[64,3200]{1,0:T(8,128)(2,1)S(1)}, bf16[64,3200]{1,0:T(8,128)(2,1)S(1)}, u32[]{:S(2)}, u32[]{:S(2)}) collective-permute-start(bf16[64,3200]{1,0:T(8,128)(2,1)S(1)} %shard_map.77), channel_id=1, source_target_pairs={{0,32},{16,240},{32,64},{48,16},{64,96},{80,48},{96,128},{112,80},... | collective-permute-start | bytes 1228808 | tf_op jit(solution)/shard_map/ppermute | solution.py:32
  57.2 2.0 %collective-permute-start.19 = (bf16[64,3200]{1,0:T(8,128)(2,1)S(1)}, bf16[64,3200]{1,0:T(8,128)(2,1)S(1)}, u32[]{:S(2)}, u32[]{:S(2)}) collective-permute-start(bf16[64,3200]{1,0:T(8,128)(2,1)S(1)} %shard_map.83), channel_id=1, source_target_pairs={{0,32},{16,240},{32,64},{48,16},{64,96},{80,48},{96,128},{112,80},... | collective-permute-start | bytes 1228808 | tf_op jit(solution)/shard_map/ppermute | solution.py:32
  59.2 2.7 %collective-permute-done.9.moving = bf16[64,3200]{1,0:T(8,128)(2,1)S(1)} collective-permute-done((bf16[64,3200]{1,0:T(8,128)(2,1)S(1)}, bf16[64,3200]{1,0:T(8,128)(2,1)S(1)}, u32[]{:S(2)}, u32[]{:S(2)}) %collective-permute-start.9) | collective-permute-done | bytes 409632 | tf_op jit(solution)/shard_map/ppermute | solution.py:32
  62.1 3.2 %collective-permute-start.10 = (bf16[64,3200]{1,0:T(8,128)(2,1)S(1)}, bf16[64,3200]{1,0:T(8,128)(2,1)S(1)}, u32[]{:S(2)}, u32[]{:S(2)}) collective-permute-start(bf16[64,3200]{1,0:T(8,128)(2,1)S(1)} %shard_map.78), channel_id=1, source_target_pairs={{0,32},{16,240},{32,64},{48,16},{64,96},{80,48},{96,128},{112,80},... | collective-permute-start | bytes 1228808 | tf_op jit(solution)/shard_map/ppermute | solution.py:32
  66.5 3.2 %collective-permute-start.20 = (bf16[64,3200]{1,0:T(8,128)(2,1)S(1)}, bf16[64,3200]{1,0:T(8,128)(2,1)S(1)}, u32[]{:S(2)}, u32[]{:S(2)}) collective-permute-start(bf16[64,3200]{1,0:T(8,128)(2,1)S(1)} %shard_map.84), channel_id=1, source_target_pairs={{0,32},{16,240},{32,64},{48,16},{64,96},{80,48},{96,128},{112,80},... | collective-permute-start | bytes 1228808 | tf_op jit(solution)/shard_map/ppermute | solution.py:32
  70.9 3.2 %collective-permute-start.11 = (bf16[64,3200]{1,0:T(8,128)(2,1)S(1)}, bf16[64,3200]{1,0:T(8,128)(2,1)S(1)}, u32[]{:S(2)}, u32[]{:S(2)}) collective-permute-start(bf16[64,3200]{1,0:T(8,128)(2,1)S(1)} %shard_map.79), channel_id=1, source_target_pairs={{0,32},{16,240},{32,64},{48,16},{64,96},{80,48},{96,128},{112,80},... | collective-permute-start | bytes 1228808 | tf_op jit(solution)/shard_map/ppermute | solution.py:32
  75.3 3.2 %collective-permute-start.21 = (bf16[64,3200]{1,0:T(8,128)(2,1)S(1)}, bf16[64,3200]{1,0:T(8,128)(2,1)S(1)}, u32[]{:S(2)}, u32[]{:S(2)}) collective-permute-start(bf16[64,3200]{1,0:T(8,128)(2,1)S(1)} %shard_map.85), channel_id=1, source_target_pairs={{0,32},{16,240},{32,64},{48,16},{64,96},{80,48},{96,128},{112,80},... | collective-permute-start | bytes 1228808 | tf_op jit(solution)/shard_map/ppermute | solution.py:32
  79.6 4.3 %collective-permute-start.12 = (bf16[32,3200]{1,0:T(8,128)(2,1)S(1)}, bf16[32,3200]{1,0:T(8,128)(2,1)S(1)}, u32[]{:S(2)}, u32[]{:S(2)}) collective-permute-start(bf16[32,3200]{1,0:T(8,128)(2,1)S(1)} %shard_map.80), channel_id=1, source_target_pairs={{0,16},{16,0},{1,17},{17,1},{2,18},{18,2},{3,19},{19,3},{4,20},{20... | collective-permute-start | bytes 614408 | tf_op jit(solution)/shard_map/ppermute | solution.py:24
  84.0 4.3 %collective-permute-start.22 = (bf16[32,3200]{1,0:T(8,128)(2,1)S(1)}, bf16[32,3200]{1,0:T(8,128)(2,1)S(1)}, u32[]{:S(2)}, u32[]{:S(2)}) collective-permute-start(bf16[32,3200]{1,0:T(8,128)(2,1)S(1)} %shard_map.86), channel_id=1, source_target_pairs={{0,16},{16,0},{1,17},{17,1},{2,18},{18,2},{3,19},{19,3},{4,20},{20... | collective-permute-start | bytes 614408 | tf_op jit(solution)/shard_map/ppermute | solution.py:24
  93.4 5.8 %collective-permute-done.14.refs_3_ = bf16[64,3072]{1,0:T(8,128)(2,1)S(1)} collective-permute-done((bf16[64,3072]{1,0:T(8,128)(2,1)S(1)}, bf16[64,3072]{1,0:T(8,128)(2,1)S(1)}, u32[]{:S(2)}, u32[]{:S(2)}) %collective-permute-start.14) | collective-permute-done | bytes 393248 | tf_op jit(solution)/shard_map/ppermute | solution.py:32
  100.2 3.3 %collective-permute-done.24.refs_8_ = bf16[64,3072]{1,0:T(8,128)(2,1)S(1)} collective-permute-done((bf16[64,3072]{1,0:T(8,128)(2,1)S(1)}, bf16[64,3072]{1,0:T(8,128)(2,1)S(1)}, u32[]{:S(2)}, u32[]{:S(2)}) %collective-permute-start.24) | collective-permute-done | bytes 393248 | tf_op jit(solution)/shard_map/ppermute | solution.py:32
  105.6 2.1 %collective-permute-done.15.refs_4_ = bf16[64,3072]{1,0:T(8,128)(2,1)S(1)} collective-permute-done((bf16[64,3072]{1,0:T(8,128)(2,1)S(1)}, bf16[64,3072]{1,0:T(8,128)(2,1)S(1)}, u32[]{:S(2)}, u32[]{:S(2)}) %collective-permute-start.15) | collective-permute-done | bytes 393248 | tf_op jit(solution)/shard_map/ppermute | solution.py:32
  107.7 2.7 %collective-permute-start.17 = (bf16[64,3072]{1,0:T(8,128)(2,1)S(1)}, bf16[64,3072]{1,0:T(8,128)(2,1)S(1)}, u32[]{:S(2)}, u32[]{:S(2)}) collective-permute-start(bf16[64,3072]{1,0:T(8,128)(2,1)S(1)} %collective-permute-done.15.refs_4_), channel_id=1, source_target_pairs={{0,16},{16,0},{1,17},{17,1},{2,18},{18,2},{3,19},{19,3},{4,20},{20... | collective-permute-start | bytes 1179656 | tf_op jit(solution)/shard_map/ppermute | solution.py:24
  111.9 2.7 %collective-permute-start.27 = (bf16[64,3072]{1,0:T(8,128)(2,1)S(1)}, bf16[64,3072]{1,0:T(8,128)(2,1)S(1)}, u32[]{:S(2)}, u32[]{:S(2)}) collective-permute-start(bf16[64,3072]{1,0:T(8,128)(2,1)S(1)} %collective-permute-done.25.refs_9_), channel_id=1, source_target_pairs={{0,16},{16,0},{1,17},{17,1},{2,18},{18,2},{3,19},{19,3},{4,20},{20... | collective-permute-start | bytes 1179656 | tf_op jit(solution)/shard_map/ppermute | solution.py:24
  115.9 4.8 %shard_map.89.refs_0_ = bf16[16,5,8,768]{3,2,1,0:T(8,128)(2,1)} custom-call(s32[2]{0:T(128)S(1)} %pad_add_fusion.place.refs_0_, bf16[3072,768]{1,0:T(8,128)(2,1)S(1)} %bitcast.9, bf16[64,3072]{1,0:T(8,128)(2,1)S(1)} %pad_maximum_fusion.refs_2_, bf16[64,3072]{1,0:T(8,128)(2,1)S(1)} %collective-permute-done.14.refs_3_, ...), custom_call_target="tpu_custom_call" | custom-call | flops 3019898880 | bytes 9633792 | tf_op jit(solution)/shard_map/pallas_call | solution.py:371
  120.7 3.6 %all-to-all-start.1 = ((bf16[16,5,8,768]{3,2,1,0:T(8,128)(2,1)}), bf16[16,5,8,768]{3,2,1,0:T(8,128)(2,1)S(1)}, u32[]{:S(2)}, u32[]{:S(2)}) async-start(bf16[16,5,8,768]{3,2,1,0:T(8,128)(2,1)} %shard_map.89.refs_0_), calls=%async_computation.1 | async-start | bytes 1966080 | tf_op jit(solution)/shard_map/all_to_all | solution.py:429
  125.8 2.1 %collective-permute-start.31 = (bf16[64,3072]{1,0:T(8,128)(2,1)S(1)}, bf16[64,3072]{1,0:T(8,128)(2,1)S(1)}, u32[]{:S(2)}, u32[]{:S(2)}) collective-permute-start(bf16[64,3072]{1,0:T(8,128)(2,1)S(1)} %collective-permute-done.30.refs_2_.value), channel_id=1, source_target_pairs={{0,16},{16,0},{1,17},{17,1},{2,18},{18,2},{3,19},{19,3},{4,20},{20... | collective-permute-start | bytes 1179656 | tf_op jit(solution)/shard_map/ppermute | solution.py:24
  129.2 2.3 %copy-done.2 = bf16[3072,768]{1,0:T(8,128)(2,1)S(1)} copy-done((bf16[3072,768]{1,0:T(8,128)(2,1)S(1)}, bf16[3072,768]{1,0:T(8,128)(2,1)}, u32[]{:S(2)}) %copy-start.2) | copy-done | bytes 4718616
  131.6 2.0 %shard_map.90 = (bf16[256,768]{1,0:T(8,128)(2,1)S(1)}, bf16[3072,768]{1,0:T(8,128)(2,1)S(1)}) custom-call(bf16[64,3072]{1,0:T(8,128)(2,1)S(1)} %collective-permute-done.28.refs_0_.value, bf16[64,3072]{1,0:T(8,128)(2,1)S(1)} %collective-permute-done.29.refs_1_, bf16[64,3072]{1,0:T(8,128)(2,1)S(1)} %collective-permute-done.30.refs_2_.value, ...), custom_call_target="tpu_custom_call" | custom-call | flops 1207959552 | bytes 6684672 | tf_op jit(solution)/shard_map/pallas_call | solution.py:351
  135.0 2.1 %collective-permute-start.35 = (bf16[32,3072]{1,0:T(8,128)(2,1)S(1)}, bf16[32,3072]{1,0:T(8,128)(2,1)S(1)}, u32[]{:S(2)}, u32[]{:S(2)}) collective-permute-start(bf16[32,3072]{1,0:T(8,128)(2,1)S(1)} %shard_map.94.refs_5_), channel_id=1, source_target_pairs={{0,16},{16,0},{1,17},{17,1},{2,18},{18,2},{3,19},{19,3},{4,20},{20... | collective-permute-start | bytes 589832 | tf_op jit(solution)/shard_map/ppermute | solution.py:24
  140.4 15.9 %all_to_all.15.far = bf16[16,3,8,768]{3,2,1,0:T(8,128)(2,1)S(1)} all-to-all(bf16[16,3,8,768]{3,2,1,0:T(8,128)(2,1)S(1)} %shard_map.95), channel_id=1, replica_groups=mesh['z'=8,'core'=2,'y'=4,'x'=4] {'y','x'}, dimensions={0} | all-to-all | bytes 1179648 | tf_op jit(solution)/shard_map/all_to_all | solution.py:429
  (99 shorter events, 34.5 us)
Async XLA Ops:
  2.2 31.8 %all-to-all-start = ((bf16[16,8,8,768]{3,2,1,0:T(8,128)(2,1)}), bf16[16,8,8,768]{3,2,1,0:T(8,128)(2,1)S(1)}, u32[]{:S(2)}, u32[]{:S(2)}) async-start(bf16[16,8,8,768]{3,2,1,0:T(8,128)(2,1)} %broadcast_in_dim.11.refs_0_), calls=%async_computation | async-start | bytes 3145728 | tf_op jit(solution)/shard_map/all_to_all | solution.py:429
  15.4 14.2 %collective-permute-start.3 = (f32[2,2,3072]{2,1,0:T(2,128)S(1)}, f32[2,2,3072]{2,1,0:T(2,128)S(1)}, u32[]{:S(2)}, u32[]{:S(2)}) collective-permute-start(f32[2,2,3072]{2,1,0:T(2,128)S(1)} %pad_maximum_fusion.3.refs_0_), channel_id=1, source_target_pairs={{0,96},{16,176},{32,128},{48,208},{64,160},{80,240},{96,192},{112,... | collective-permute-start | bytes 147464 | tf_op jit(solution)/shard_map/ppermute | solution.py:32
  21.9 7.6 %collective-permute-start.2 = (f32[2,2,3072]{2,1,0:T(2,128)S(1)}, f32[2,2,3072]{2,1,0:T(2,128)S(1)}, u32[]{:S(2)}, u32[]{:S(2)}) collective-permute-start(f32[2,2,3072]{2,1,0:T(2,128)S(1)} %pad_maximum_fusion.3.refs_0_), channel_id=1, source_target_pairs={{0,64},{16,208},{32,96},{48,240},{64,128},{80,16},{96,160},{112,48... | collective-permute-start | bytes 147464 | tf_op jit(solution)/shard_map/ppermute | solution.py:32
  22.2 7.4 %collective-permute-start.1 = (f32[2,2,3072]{2,1,0:T(2,128)S(1)}, f32[2,2,3072]{2,1,0:T(2,128)S(1)}, u32[]{:S(2)}, u32[]{:S(2)}) collective-permute-start(f32[2,2,3072]{2,1,0:T(2,128)S(1)} %pad_maximum_fusion.3.refs_0_), channel_id=1, source_target_pairs={{0,32},{16,240},{32,64},{48,16},{64,96},{80,48},{96,128},{112,80},... | collective-permute-start | bytes 147464 | tf_op jit(solution)/shard_map/ppermute | solution.py:32
  22.7 6.9 %collective-permute-start.4 = (f32[2,3072]{1,0:T(2,128)S(1)}, f32[2,3072]{1,0:T(2,128)S(1)}, u32[]{:S(2)}, u32[]{:S(2)}) collective-permute-start(f32[2,3072]{1,0:T(2,128)S(1)} %shard_map.73), channel_id=1, source_target_pairs={{0,128},{16,144},{32,160},{48,176},{64,192},{80,208},{96,224},{112... | collective-permute-start | bytes 73736 | tf_op jit(solution)/shard_map/ppermute | solution.py:32
  29.7 4.3 %collective-permute-start.5 = (f32[7,2,3072]{2,1,0:T(2,128)S(1)}, f32[7,2,3072]{2,1,0:T(2,128)S(1)}, u32[]{:S(2)}, u32[]{:S(2)}) collective-permute-start(f32[7,2,3072]{2,1,0:T(2,128)S(1)} %pad_maximum_fusion.2.refs_1_), channel_id=1, source_target_pairs={{0,16},{16,0},{1,17},{17,1},{2,18},{18,2},{3,19},{19,3},{4,20},{20... | collective-permute-start | bytes 516104 | tf_op jit(solution)/shard_map/ppermute | solution.py:24
  39.2 6.0 %collective-permute-start.7 = (bf16[192,3200]{1,0:T(8,128)(2,1)S(1)}, bf16[192,3200]{1,0:T(8,128)(2,1)S(1)}, u32[]{:S(2)}, u32[]{:S(2)}) collective-permute-start(bf16[192,3200]{1,0:T(8,128)(2,1)S(1)} %get-tuple-element.11.refs_0_), channel_id=1, source_target_pairs={{0,16},{16,0},{1,17},{17,1},{2,18},{18,2},{3,19},{19,3},{4,20},{20... | collective-permute-start | bytes 3686408 | tf_op jit(solution)/shard_map/ppermute | solution.py:24
  45.1 14.1 %collective-permute-start.6 = (bf16[256,3200]{1,0:T(8,128)(2,1)S(1)}, bf16[256,3200]{1,0:T(8,128)(2,1)S(1)}, u32[]{:S(2)}, u32[]{:S(2)}) collective-permute-start(bf16[256,3200]{1,0:T(8,128)(2,1)S(1)} %get-tuple-element.13), channel_id=1, source_target_pairs={{0,16},{16,0},{1,17},{17,1},{2,18},{18,2},{3,19},{19,3},{4,20},{20... | collective-permute-start | bytes 4915208 | tf_op jit(solution)/shard_map/ppermute | solution.py:24
  45.3 8.4 %collective-permute-start.8 = (bf16[32,3200]{1,0:T(8,128)(2,1)S(1)}, bf16[32,3200]{1,0:T(8,128)(2,1)S(1)}, u32[]{:S(2)}, u32[]{:S(2)}) collective-permute-start(bf16[32,3200]{1,0:T(8,128)(2,1)S(1)} %shard_map.76), channel_id=1, source_target_pairs={{0,32},{16,240},{32,64},{48,16},{64,96},{80,48},{96,128},{112,80},... | collective-permute-start | bytes 614408 | tf_op jit(solution)/shard_map/ppermute | solution.py:32
  51.1 6.0 %collective-permute-start.18 = (bf16[32,3200]{1,0:T(8,128)(2,1)S(1)}, bf16[32,3200]{1,0:T(8,128)(2,1)S(1)}, u32[]{:S(2)}, u32[]{:S(2)}) collective-permute-start(bf16[32,3200]{1,0:T(8,128)(2,1)S(1)} %shard_map.82), channel_id=1, source_target_pairs={{0,32},{16,240},{32,64},{48,16},{64,96},{80,48},{96,128},{112,80},... | collective-permute-start | bytes 614408 | tf_op jit(solution)/shard_map/ppermute | solution.py:32
  53.8 8.1 %collective-permute-start.9 = (bf16[64,3200]{1,0:T(8,128)(2,1)S(1)}, bf16[64,3200]{1,0:T(8,128)(2,1)S(1)}, u32[]{:S(2)}, u32[]{:S(2)}) collective-permute-start(bf16[64,3200]{1,0:T(8,128)(2,1)S(1)} %shard_map.77), channel_id=1, source_target_pairs={{0,32},{16,240},{32,64},{48,16},{64,96},{80,48},{96,128},{112,80},... | collective-permute-start | bytes 1228808 | tf_op jit(solution)/shard_map/ppermute | solution.py:32
  57.2 9.1 %collective-permute-start.19 = (bf16[64,3200]{1,0:T(8,128)(2,1)S(1)}, bf16[64,3200]{1,0:T(8,128)(2,1)S(1)}, u32[]{:S(2)}, u32[]{:S(2)}) collective-permute-start(bf16[64,3200]{1,0:T(8,128)(2,1)S(1)} %shard_map.83), channel_id=1, source_target_pairs={{0,32},{16,240},{32,64},{48,16},{64,96},{80,48},{96,128},{112,80},... | collective-permute-start | bytes 1228808 | tf_op jit(solution)/shard_map/ppermute | solution.py:32
  62.1 8.6 %collective-permute-start.10 = (bf16[64,3200]{1,0:T(8,128)(2,1)S(1)}, bf16[64,3200]{1,0:T(8,128)(2,1)S(1)}, u32[]{:S(2)}, u32[]{:S(2)}) collective-permute-start(bf16[64,3200]{1,0:T(8,128)(2,1)S(1)} %shard_map.78), channel_id=1, source_target_pairs={{0,32},{16,240},{32,64},{48,16},{64,96},{80,48},{96,128},{112,80},... | collective-permute-start | bytes 1228808 | tf_op jit(solution)/shard_map/ppermute | solution.py:32
  66.5 8.6 %collective-permute-start.20 = (bf16[64,3200]{1,0:T(8,128)(2,1)S(1)}, bf16[64,3200]{1,0:T(8,128)(2,1)S(1)}, u32[]{:S(2)}, u32[]{:S(2)}) collective-permute-start(bf16[64,3200]{1,0:T(8,128)(2,1)S(1)} %shard_map.84), channel_id=1, source_target_pairs={{0,32},{16,240},{32,64},{48,16},{64,96},{80,48},{96,128},{112,80},... | collective-permute-start | bytes 1228808 | tf_op jit(solution)/shard_map/ppermute | solution.py:32
  70.9 8.6 %collective-permute-start.11 = (bf16[64,3200]{1,0:T(8,128)(2,1)S(1)}, bf16[64,3200]{1,0:T(8,128)(2,1)S(1)}, u32[]{:S(2)}, u32[]{:S(2)}) collective-permute-start(bf16[64,3200]{1,0:T(8,128)(2,1)S(1)} %shard_map.79), channel_id=1, source_target_pairs={{0,32},{16,240},{32,64},{48,16},{64,96},{80,48},{96,128},{112,80},... | collective-permute-start | bytes 1228808 | tf_op jit(solution)/shard_map/ppermute | solution.py:32
  75.3 8.6 %collective-permute-start.21 = (bf16[64,3200]{1,0:T(8,128)(2,1)S(1)}, bf16[64,3200]{1,0:T(8,128)(2,1)S(1)}, u32[]{:S(2)}, u32[]{:S(2)}) collective-permute-start(bf16[64,3200]{1,0:T(8,128)(2,1)S(1)} %shard_map.85), channel_id=1, source_target_pairs={{0,32},{16,240},{32,64},{48,16},{64,96},{80,48},{96,128},{112,80},... | collective-permute-start | bytes 1228808 | tf_op jit(solution)/shard_map/ppermute | solution.py:32
  79.6 8.7 %collective-permute-start.12 = (bf16[32,3200]{1,0:T(8,128)(2,1)S(1)}, bf16[32,3200]{1,0:T(8,128)(2,1)S(1)}, u32[]{:S(2)}, u32[]{:S(2)}) collective-permute-start(bf16[32,3200]{1,0:T(8,128)(2,1)S(1)} %shard_map.80), channel_id=1, source_target_pairs={{0,16},{16,0},{1,17},{17,1},{2,18},{18,2},{3,19},{19,3},{4,20},{20... | collective-permute-start | bytes 614408 | tf_op jit(solution)/shard_map/ppermute | solution.py:24
  84.0 6.1 %collective-permute-start.22 = (bf16[32,3200]{1,0:T(8,128)(2,1)S(1)}, bf16[32,3200]{1,0:T(8,128)(2,1)S(1)}, u32[]{:S(2)}, u32[]{:S(2)}) collective-permute-start(bf16[32,3200]{1,0:T(8,128)(2,1)S(1)} %shard_map.86), channel_id=1, source_target_pairs={{0,16},{16,0},{1,17},{17,1},{2,18},{18,2},{3,19},{19,3},{4,20},{20... | collective-permute-start | bytes 614408 | tf_op jit(solution)/shard_map/ppermute | solution.py:24
  92.2 7.0 %collective-permute-start.14 = (bf16[64,3072]{1,0:T(8,128)(2,1)S(1)}, bf16[64,3072]{1,0:T(8,128)(2,1)S(1)}, u32[]{:S(2)}, u32[]{:S(2)}) collective-permute-start(bf16[64,3072]{1,0:T(8,128)(2,1)S(1)} %pad_maximum_fusion.refs_2_), channel_id=1, source_target_pairs={{0,32},{16,240},{32,64},{48,16},{64,96},{80,48},{96,128},{112,80},... | collective-permute-start | bytes 1179656 | tf_op jit(solution)/shard_map/ppermute | solution.py:32
  93.3 10.1 %collective-permute-start.24 = (bf16[64,3072]{1,0:T(8,128)(2,1)S(1)}, bf16[64,3072]{1,0:T(8,128)(2,1)S(1)}, u32[]{:S(2)}, u32[]{:S(2)}) collective-permute-start(bf16[64,3072]{1,0:T(8,128)(2,1)S(1)} %pad_maximum_fusion.1.refs_7_), channel_id=1, source_target_pairs={{0,32},{16,240},{32,64},{48,16},{64,96},{80,48},{96,128},{112,80},... | collective-permute-start | bytes 1179656 | tf_op jit(solution)/shard_map/ppermute | solution.py:32
  99.2 8.4 %collective-permute-start.15 = (bf16[64,3072]{1,0:T(8,128)(2,1)S(1)}, bf16[64,3072]{1,0:T(8,128)(2,1)S(1)}, u32[]{:S(2)}, u32[]{:S(2)}) collective-permute-start(bf16[64,3072]{1,0:T(8,128)(2,1)S(1)} %collective-permute-done.14.refs_3_), channel_id=1, source_target_pairs={{0,32},{16,240},{32,64},{48,16},{64,96},{80,48},{96,128},{112,80},... | collective-permute-start | bytes 1179656 | tf_op jit(solution)/shard_map/ppermute | solution.py:32
  103.5 8.4 %collective-permute-start.25 = (bf16[64,3072]{1,0:T(8,128)(2,1)S(1)}, bf16[64,3072]{1,0:T(8,128)(2,1)S(1)}, u32[]{:S(2)}, u32[]{:S(2)}) collective-permute-start(bf16[64,3072]{1,0:T(8,128)(2,1)S(1)} %collective-permute-done.24.refs_8_), channel_id=1, source_target_pairs={{0,32},{16,240},{32,64},{48,16},{64,96},{80,48},{96,128},{112,80},... | collective-permute-start | bytes 1179656 | tf_op jit(solution)/shard_map/ppermute | solution.py:32
  104.4 10.3 %collective-permute-start.16 = (bf16[64,3072]{1,0:T(8,128)(2,1)S(1)}, bf16[64,3072]{1,0:T(8,128)(2,1)S(1)}, u32[]{:S(2)}, u32[]{:S(2)}) collective-permute-start(bf16[64,3072]{1,0:T(8,128)(2,1)S(1)} %collective-permute-done.14.refs_3_), channel_id=1, source_target_pairs={{0,16},{16,0},{1,17},{17,1},{2,18},{18,2},{3,19},{19,3},{4,20},{20... | collective-permute-start | bytes 1179656 | tf_op jit(solution)/shard_map/ppermute | solution.py:24
  105.6 9.2 %collective-permute-start.26 = (bf16[64,3072]{1,0:T(8,128)(2,1)S(1)}, bf16[64,3072]{1,0:T(8,128)(2,1)S(1)}, u32[]{:S(2)}, u32[]{:S(2)}) collective-permute-start(bf16[64,3072]{1,0:T(8,128)(2,1)S(1)} %collective-permute-done.24.refs_8_), channel_id=1, source_target_pairs={{0,16},{16,0},{1,17},{17,1},{2,18},{18,2},{3,19},{19,3},{4,20},{20... | collective-permute-start | bytes 1179656 | tf_op jit(solution)/shard_map/ppermute | solution.py:24
  107.7 7.1 %collective-permute-start.17 = (bf16[64,3072]{1,0:T(8,128)(2,1)S(1)}, bf16[64,3072]{1,0:T(8,128)(2,1)S(1)}, u32[]{:S(2)}, u32[]{:S(2)}) collective-permute-start(bf16[64,3072]{1,0:T(8,128)(2,1)S(1)} %collective-permute-done.15.refs_4_), channel_id=1, source_target_pairs={{0,16},{16,0},{1,17},{17,1},{2,18},{18,2},{3,19},{19,3},{4,20},{20... | collective-permute-start | bytes 1179656 | tf_op jit(solution)/shard_map/ppermute | solution.py:24
  111.9 4.0 %collective-permute-start.27 = (bf16[64,3072]{1,0:T(8,128)(2,1)S(1)}, bf16[64,3072]{1,0:T(8,128)(2,1)S(1)}, u32[]{:S(2)}, u32[]{:S(2)}) collective-permute-start(bf16[64,3072]{1,0:T(8,128)(2,1)S(1)} %collective-permute-done.25.refs_9_), channel_id=1, source_target_pairs={{0,16},{16,0},{1,17},{17,1},{2,18},{18,2},{3,19},{19,3},{4,20},{20... | collective-permute-start | bytes 1179656 | tf_op jit(solution)/shard_map/ppermute | solution.py:24
  114.6 9.7 %collective-permute-start.28 = (bf16[64,3072]{1,0:T(8,128)(2,1)S(1)}, bf16[64,3072]{1,0:T(8,128)(2,1)S(1)}, u32[]{:S(2)}, u32[]{:S(2)}) collective-permute-start(bf16[64,3072]{1,0:T(8,128)(2,1)S(1)} %collective-permute-done.15.refs_4_), channel_id=1, source_target_pairs={{0,32},{16,240},{32,64},{48,16},{64,96},{80,48},{96,128},{112,80},... | collective-permute-start | bytes 1179656 | tf_op jit(solution)/shard_map/ppermute | solution.py:32
  114.7 11.1 %collective-permute-start.30 = (bf16[64,3072]{1,0:T(8,128)(2,1)S(1)}, bf16[64,3072]{1,0:T(8,128)(2,1)S(1)}, u32[]{:S(2)}, u32[]{:S(2)}) collective-permute-start(bf16[64,3072]{1,0:T(8,128)(2,1)S(1)} %collective-permute-done.25.refs_9_), channel_id=1, source_target_pairs={{0,32},{16,240},{32,64},{48,16},{64,96},{80,48},{96,128},{112,80},... | collective-permute-start | bytes 1179656 | tf_op jit(solution)/shard_map/ppermute | solution.py:32
  120.7 19.7 %all-to-all-start.1 = ((bf16[16,5,8,768]{3,2,1,0:T(8,128)(2,1)}), bf16[16,5,8,768]{3,2,1,0:T(8,128)(2,1)S(1)}, u32[]{:S(2)}, u32[]{:S(2)}) async-start(bf16[16,5,8,768]{3,2,1,0:T(8,128)(2,1)} %shard_map.89.refs_0_), calls=%async_computation.1 | async-start | bytes 1966080 | tf_op jit(solution)/shard_map/all_to_all | solution.py:429
  124.3 4.7 %collective-permute-start.29 = (bf16[64,3072]{1,0:T(8,128)(2,1)S(1)}, bf16[64,3072]{1,0:T(8,128)(2,1)S(1)}, u32[]{:S(2)}, u32[]{:S(2)}) collective-permute-start(bf16[64,3072]{1,0:T(8,128)(2,1)S(1)} %collective-permute-done.28.refs_0_.value), channel_id=1, source_target_pairs={{0,16},{16,0},{1,17},{17,1},{2,18},{18,2},{3,19},{19,3},{4,20},{20... | collective-permute-start | bytes 1179656 | tf_op jit(solution)/shard_map/ppermute | solution.py:24
  127.9 5.6 %collective-permute-start.32 = (bf16[32,3072]{1,0:T(8,128)(2,1)S(1)}, bf16[32,3072]{1,0:T(8,128)(2,1)S(1)}, u32[]{:S(2)}, u32[]{:S(2)}) collective-permute-start(bf16[32,3072]{1,0:T(8,128)(2,1)S(1)} %shard_map.91), channel_id=1, source_target_pairs={{0,32},{16,240},{32,64},{48,16},{64,96},{80,48},{96,128},{112,80},... | collective-permute-start | bytes 589832 | tf_op jit(solution)/shard_map/ppermute | solution.py:32
  128.0 7.0 %collective-permute-start.34 = (bf16[32,3072]{1,0:T(8,128)(2,1)S(1)}, bf16[32,3072]{1,0:T(8,128)(2,1)S(1)}, u32[]{:S(2)}, u32[]{:S(2)}) collective-permute-start(bf16[32,3072]{1,0:T(8,128)(2,1)S(1)} %shard_map.93), channel_id=1, source_target_pairs={{0,32},{16,240},{32,64},{48,16},{64,96},{80,48},{96,128},{112,80},... | collective-permute-start | bytes 589832 | tf_op jit(solution)/shard_map/ppermute | solution.py:32
  (16 other events, 154.3 us)
